TPU v7x, 256 devices: a whole 4x4x8 slice. The times are simulated.
256 devices in a mesh: section: 16 (over y, x), dp: 16 (over z, core).
Axes of the slice: x: 4, y: 4, z: 8, core: 2. Of those that a mesh axis runs over, the one named last changes fastest.
Arguments:
- acts: bfloat16 [16, 1, 2048, 4608], P('section', None, 'dp'), may hold values from -6 to 6
- output_gradient: bfloat16 [1, 2048, 4608], P(None, 'dp'), may hold values from -6 to 6
- gains: float32 [16, 4608], P('section'), may hold values from 0.5 to 1.5
- adapter_down_weight: bfloat16 [16, 4608, 128], P('section'), may hold values from -0.5 to 0.5
- adapter_up_weight: bfloat16 [16, 4608, 128], P('section'), may hold values from -0.5 to 0.5
- thresholds: float32 [16, 1, 64], P('section'), may hold values from 10 to 40
- document_lengths: int32 [1, 64], replicated, may hold values from 1 to 64, 2048 in all within a row
- owners: int32 [1, 64], replicated, may hold values from 0 to 15, as said below
Outputs:
- input_grads: bfloat16 [16, 1, 2048, 4608], P('section', None, 'dp')
- lora_grad: float32 [16, 4608, 256], P('section', 'dp')
- owned_ratios: float32 [16, 1, 128], P('section', None, 'dp')
Inputs may be any that keep to these rules, and one draw needn't show every extreme that they name: `document_lengths`: each row sums to 2048; its longest document has exactly 64 tokens. `owners`: in each row no device owns more than 8 documents, and some device owns exactly 8.
All inputs are finite; a program needn't handle non-finite values.
Results may differ from a plain program's by a relative error of at most 0.019.
Values may be sent and summed in bfloat16 or wider, within the bound.
A program may use at most 64 MiB of HBM per device.

v0:
```python
import jax
import jax.numpy as jnp
from jax import lax
from jax.sharding import PartitionSpec as P

OWN = 8


NORM_EPS = 1e-06
HIGHEST_PRECISION = lax.Precision.HIGHEST


def passed_along(value, axis, steps):
    count = lax.axis_size(axis)
    leading, last = (max(0, -steps), min(count, count - steps))
    return lax.ppermute(value, axis, [(source, source + steps) for source in range(leading, last)])


def section_back(layer_inputs, incoming_gradient, norm_gain, down_matrix, up_matrix):
    wide_layer_inputs = layer_inputs.astype(jnp.float32)
    clip_scale = lax.rsqrt(
        jnp.mean(wide_layer_inputs * wide_layer_inputs, axis=-1, keepdims=True) + NORM_EPS
    )
    centered_input = wide_layer_inputs * clip_scale
    low_rank = jnp.dot(incoming_gradient, up_matrix, preferred_element_type=jnp.float32).astype(
        jnp.bfloat16
    )
    back = lax.dot_general(
        low_rank, down_matrix, (((1,), (1,)), ((), ())), preferred_element_type=jnp.float32
    )
    scaled_gradient = back * norm_gain
    final_result = incoming_gradient.astype(jnp.float32) + clip_scale * (
        scaled_gradient
        - centered_input * jnp.mean(scaled_gradient * centered_input, axis=-1, keepdims=True)
    )
    return (final_result.astype(jnp.bfloat16), low_rank)


def token_gram(left_rows, right_rows):
    return jnp.einsum("mtf,msf->mts", left_rows, right_rows, preferred_element_type=jnp.float32)


def on_device(
    acts,
    output_gradient,
    gains,
    adapter_down_weight,
    adapter_up_weight,
    thresholds,
    document_lengths,
    owners,
):
    section_count = lax.axis_size("section")
    section_index = lax.axis_index("section")
    layer_inputs = acts[0]
    norm_gain = gains[0]
    down_matrix = adapter_down_weight[0]
    up_matrix = adapter_up_weight[0]
    sequence_total, seq_rows, feature_width = layer_inputs.shape
    rank_width = down_matrix.shape[1]
    document_total = document_lengths.shape[1]
    split_factor = 1
    piece_count = sequence_total * split_factor
    piece_rows = seq_rows // split_factor

    def chain_tick(tick, carry):
        incoming, arrived, arrived_low, outgoing_gradient = carry
        slot_raw = tick - (section_count - 1 - section_index)
        is_valid = (slot_raw >= 0) & (slot_raw < piece_count)
        slot_pos = jnp.clip(slot_raw, 0, piece_count - 1)
        from_top = lax.dynamic_index_in_dim(output_gradient, slot_pos, 0, keepdims=False)
        incoming_gradient = jnp.where(section_index == section_count - 1, from_top, incoming)
        piece_in = lax.dynamic_index_in_dim(layer_inputs, slot_pos, 0, keepdims=False)
        final_result, low_rank = section_back(
            piece_in, incoming_gradient, norm_gain, down_matrix, up_matrix
        )
        old_arrived = lax.dynamic_index_in_dim(arrived, slot_pos, 0, keepdims=False)
        arrived = lax.dynamic_update_index_in_dim(
            arrived, jnp.where(is_valid, incoming_gradient, old_arrived), slot_pos, 0
        )
        old_low = lax.dynamic_index_in_dim(arrived_low, slot_pos, 0, keepdims=False)
        arrived_low = lax.dynamic_update_index_in_dim(
            arrived_low, jnp.where(is_valid, low_rank, old_low), slot_pos, 0
        )
        old_leaving = lax.dynamic_index_in_dim(outgoing_gradient, slot_pos, 0, keepdims=False)
        outgoing_gradient = lax.dynamic_update_index_in_dim(
            outgoing_gradient, jnp.where(is_valid, final_result, old_leaving), slot_pos, 0
        )
        incoming = passed_along(final_result, "section", -1)
        return (incoming, arrived, arrived_low, outgoing_gradient)

    start_carry = (
        jnp.zeros((piece_rows, feature_width), jnp.bfloat16),
        jnp.zeros((piece_count, piece_rows, feature_width), jnp.bfloat16),
        jnp.zeros((piece_count, piece_rows, rank_width), jnp.bfloat16),
        jnp.zeros((piece_count, piece_rows, feature_width), jnp.bfloat16),
    )
    final_carry = lax.fori_loop(0, piece_count + section_count - 1, chain_tick, start_carry)
    incoming_gradient = final_carry[1]
    low_rank = final_carry[2]
    outgoing_gradient = final_carry[3]
    wide_layer_inputs = layer_inputs.astype(jnp.float32)
    clip_scale = lax.rsqrt(
        jnp.mean(wide_layer_inputs * wide_layer_inputs, axis=-1, keepdims=True) + NORM_EPS
    )
    normalized_input = (wide_layer_inputs * clip_scale * norm_gain).astype(jnp.bfloat16)
    hidden = jnp.einsum(
        "mtd,dr->mtr", normalized_input, down_matrix, preferred_element_type=jnp.float32
    ).astype(jnp.bfloat16)
    span_rows = seq_rows // 2
    next_normed, next_arriving, next_low, next_hidden = passed_along(
        (
            normalized_input[:, :span_rows],
            incoming_gradient[:, :span_rows],
            low_rank[:, :span_rows],
            hidden[:, :span_rows],
        ),
        "dp",
        -1,
    )
    kernel = token_gram(
        normalized_input, jnp.concatenate([normalized_input, next_normed], axis=1)
    ) * token_gram(low_rank, jnp.concatenate([low_rank, next_low], axis=1))
    kernel = kernel + token_gram(
        hidden, jnp.concatenate([hidden, next_hidden], axis=1)
    ) * token_gram(incoming_gradient, jnp.concatenate([incoming_gradient, next_arriving], axis=1))
    shard_index = lax.axis_index("dp")
    seq_ends = jnp.cumsum(document_lengths, axis=1)
    column_ids = jnp.arange(seq_rows + span_rows, dtype=jnp.int32)
    positions = shard_index * seq_rows + column_ids
    doc_ids = jnp.sum((seq_ends[:, None, :] <= positions[None, :, None]).astype(jnp.int32), axis=2)
    column_weight = jnp.where(column_ids < seq_rows, 1.0, 2.0).astype(jnp.float32)
    weight = jnp.where(doc_ids[:, :seq_rows, None] == doc_ids[:, None, :], column_weight, 0.0)
    row_sums = jnp.sum(kernel * weight, axis=2)
    doc_range = jnp.arange(document_total, dtype=jnp.int32)
    one_hot = (doc_ids[:, :seq_rows, None] == doc_range[None, None, :]).astype(jnp.float32)
    partial_sums = jnp.einsum("mt,mtk->mk", row_sums, one_hot, precision=HIGHEST_PRECISION)
    pair_sum = lax.psum(partial_sums, "dp")
    ratio = jnp.sqrt(pair_sum / (feature_width * rank_width) + NORM_EPS) / thresholds[0]
    clip_bound = jnp.minimum(1.0, 1.0 / ratio)
    token_clip = jnp.einsum("mtk,mk->mt", one_hot, clip_bound, precision=HIGHEST_PRECISION)
    weighted_low = (token_clip[..., None] * low_rank.astype(jnp.float32)).astype(jnp.bfloat16)
    weighted_hidden = (token_clip[..., None] * hidden.astype(jnp.float32)).astype(jnp.bfloat16)
    flat_rows = sequence_total * seq_rows
    normed_flat = normalized_input.reshape(flat_rows, feature_width)
    arriving_flat = incoming_gradient.reshape(flat_rows, feature_width)
    low_flat = weighted_low.reshape(flat_rows, rank_width)
    hidden_flat = weighted_hidden.reshape(flat_rows, rank_width)
    down_gradient = lax.dot_general(
        normed_flat, low_flat, (((0,), (0,)), ((), ())), preferred_element_type=jnp.float32
    )
    up_gradient = lax.dot_general(
        arriving_flat, hidden_flat, (((0,), (0,)), ((), ())), preferred_element_type=jnp.float32
    )
    document_summed = lax.psum_scatter(
        jnp.concatenate([down_gradient, up_gradient], axis=1).astype(jnp.bfloat16),
        "dp",
        scatter_dimension=0,
        tiled=True,
    ).astype(jnp.float32)
    adapter_slice = document_summed / (sequence_total * document_total)
    mine = (owners == shard_index).astype(jnp.int32)
    rank_of = jnp.cumsum(mine, axis=1) - 1
    slot_ids = jnp.arange(OWN, dtype=jnp.int32)
    picked = jnp.where((mine[..., None] == 1) & (rank_of[..., None] == slot_ids), 1.0, 0.0).astype(
        jnp.float32
    )
    held_slice = jnp.einsum("mk,mkj->mj", ratio, picked, precision=HIGHEST_PRECISION)
    return (outgoing_gradient[None], adapter_slice[None], held_slice[None])


def solution(mesh):
    placed = (
        P("section", None, "dp", None),
        P(None, "dp", None),
        P("section", None),
        P("section", None, None),
        P("section", None, None),
        P("section", None, None),
        P(),
        P(),
    )
    return jax.shard_map(
        on_device,
        mesh=mesh,
        in_specs=placed,
        out_specs=(
            P("section", None, "dp", None),
            P("section", "dp", None),
            P("section", None, "dp"),
        ),
        check_vma=False,
    )
```

profile of v0, /device:TPU:1, one launch (start us, length us, event | category | flops | bytes accessed | tf_op | source)
XLA Modules:
  0.0 717.8 jit_solution(11829914588433248951)
XLA Ops:
  10.1 560.9 %while.21 = (s32[]{:T(128)}, bf16[128,4608]{1,0:T(8,128)(2,1)}, bf16[1,128,4608]{2,1,0:T(8,128)(2,1)S(1)}, bf16[1,128,128]{2,1,0:T(8,128)(2,1)}, bf16[1,128,4608...) while((s32[]{:T(128)}, bf16[128,4608]{1,0:T(8,128)(2,1)}, ...), condition=%wide.region_3.4_spmd, body=%wide.region_0.3_spmd.sunk | while | flops 313229440 | bytes 46230348 | solution.py:98
  10.5 2.3 fusion.76
  22.9 24.8 %collective-permute-done = bf16[128,4608]{1,0:T(8,128)(2,1)S(1)} collective-permute-done((bf16[128,4608]{1,0:T(8,128)(2,1)}, bf16[128,4608]{1,0:T(8,128)(2,1)S(1)}, u32[]{:S(2)}, u32[]{:S(2)}) %collective-permute-start) | collective-permute-done | bytes 1179680 | tf_op jit(solution)/shard_map/while/body/eval_jaxpr/ppermute | solution.py:16
  49.1 2.3 fusion.76
  61.6 27.4 %collective-permute-done = bf16[128,4608]{1,0:T(8,128)(2,1)S(1)} collective-permute-done((bf16[128,4608]{1,0:T(8,128)(2,1)}, bf16[128,4608]{1,0:T(8,128)(2,1)S(1)}, u32[]{:S(2)}, u32[]{:S(2)}) %collective-permute-start) | collective-permute-done | bytes 1179680 | tf_op jit(solution)/shard_map/while/body/eval_jaxpr/ppermute | solution.py:16
  102.7 24.4 %collective-permute-done = bf16[128,4608]{1,0:T(8,128)(2,1)S(1)} collective-permute-done((bf16[128,4608]{1,0:T(8,128)(2,1)}, bf16[128,4608]{1,0:T(8,128)(2,1)S(1)}, u32[]{:S(2)}, u32[]{:S(2)}) %collective-permute-start) | collective-permute-done | bytes 1179680 | tf_op jit(solution)/shard_map/while/body/eval_jaxpr/ppermute | solution.py:16
  140.9 26.5 %collective-permute-done = bf16[128,4608]{1,0:T(8,128)(2,1)S(1)} collective-permute-done((bf16[128,4608]{1,0:T(8,128)(2,1)}, bf16[128,4608]{1,0:T(8,128)(2,1)S(1)}, u32[]{:S(2)}, u32[]{:S(2)}) %collective-permute-start) | collective-permute-done | bytes 1179680 | tf_op jit(solution)/shard_map/while/body/eval_jaxpr/ppermute | solution.py:16
  181.2 24.6 %collective-permute-done = bf16[128,4608]{1,0:T(8,128)(2,1)S(1)} collective-permute-done((bf16[128,4608]{1,0:T(8,128)(2,1)}, bf16[128,4608]{1,0:T(8,128)(2,1)S(1)}, u32[]{:S(2)}, u32[]{:S(2)}) %collective-permute-start) | collective-permute-done | bytes 1179680 | tf_op jit(solution)/shard_map/while/body/eval_jaxpr/ppermute | solution.py:16
  219.7 23.8 %collective-permute-done = bf16[128,4608]{1,0:T(8,128)(2,1)S(1)} collective-permute-done((bf16[128,4608]{1,0:T(8,128)(2,1)}, bf16[128,4608]{1,0:T(8,128)(2,1)S(1)}, u32[]{:S(2)}, u32[]{:S(2)}) %collective-permute-start) | collective-permute-done | bytes 1179680 | tf_op jit(solution)/shard_map/while/body/eval_jaxpr/ppermute | solution.py:16
  257.3 22.8 %collective-permute-done = bf16[128,4608]{1,0:T(8,128)(2,1)S(1)} collective-permute-done((bf16[128,4608]{1,0:T(8,128)(2,1)}, bf16[128,4608]{1,0:T(8,128)(2,1)S(1)}, u32[]{:S(2)}, u32[]{:S(2)}) %collective-permute-start) | collective-permute-done | bytes 1179680 | tf_op jit(solution)/shard_map/while/body/eval_jaxpr/ppermute | solution.py:16
  293.9 21.9 %collective-permute-done = bf16[128,4608]{1,0:T(8,128)(2,1)S(1)} collective-permute-done((bf16[128,4608]{1,0:T(8,128)(2,1)}, bf16[128,4608]{1,0:T(8,128)(2,1)S(1)}, u32[]{:S(2)}, u32[]{:S(2)}) %collective-permute-start) | collective-permute-done | bytes 1179680 | tf_op jit(solution)/shard_map/while/body/eval_jaxpr/ppermute | solution.py:16
  329.6 21.0 %collective-permute-done = bf16[128,4608]{1,0:T(8,128)(2,1)S(1)} collective-permute-done((bf16[128,4608]{1,0:T(8,128)(2,1)}, bf16[128,4608]{1,0:T(8,128)(2,1)S(1)}, u32[]{:S(2)}, u32[]{:S(2)}) %collective-permute-start) | collective-permute-done | bytes 1179680 | tf_op jit(solution)/shard_map/while/body/eval_jaxpr/ppermute | solution.py:16
  364.4 20.0 %collective-permute-done = bf16[128,4608]{1,0:T(8,128)(2,1)S(1)} collective-permute-done((bf16[128,4608]{1,0:T(8,128)(2,1)}, bf16[128,4608]{1,0:T(8,128)(2,1)S(1)}, u32[]{:S(2)}, u32[]{:S(2)}) %collective-permute-start) | collective-permute-done | bytes 1179680 | tf_op jit(solution)/shard_map/while/body/eval_jaxpr/ppermute | solution.py:16
  398.2 19.1 %collective-permute-done = bf16[128,4608]{1,0:T(8,128)(2,1)S(1)} collective-permute-done((bf16[128,4608]{1,0:T(8,128)(2,1)}, bf16[128,4608]{1,0:T(8,128)(2,1)S(1)}, u32[]{:S(2)}, u32[]{:S(2)}) %collective-permute-start) | collective-permute-done | bytes 1179680 | tf_op jit(solution)/shard_map/while/body/eval_jaxpr/ppermute | solution.py:16
  431.2 18.2 %collective-permute-done = bf16[128,4608]{1,0:T(8,128)(2,1)S(1)} collective-permute-done((bf16[128,4608]{1,0:T(8,128)(2,1)}, bf16[128,4608]{1,0:T(8,128)(2,1)S(1)}, u32[]{:S(2)}, u32[]{:S(2)}) %collective-permute-start) | collective-permute-done | bytes 1179680 | tf_op jit(solution)/shard_map/while/body/eval_jaxpr/ppermute | solution.py:16
  463.2 17.2 %collective-permute-done = bf16[128,4608]{1,0:T(8,128)(2,1)S(1)} collective-permute-done((bf16[128,4608]{1,0:T(8,128)(2,1)}, bf16[128,4608]{1,0:T(8,128)(2,1)S(1)}, u32[]{:S(2)}, u32[]{:S(2)}) %collective-permute-start) | collective-permute-done | bytes 1179680 | tf_op jit(solution)/shard_map/while/body/eval_jaxpr/ppermute | solution.py:16
  494.3 16.4 %collective-permute-done = bf16[128,4608]{1,0:T(8,128)(2,1)S(1)} collective-permute-done((bf16[128,4608]{1,0:T(8,128)(2,1)}, bf16[128,4608]{1,0:T(8,128)(2,1)S(1)}, u32[]{:S(2)}, u32[]{:S(2)}) %collective-permute-start) | collective-permute-done | bytes 1179680 | tf_op jit(solution)/shard_map/while/body/eval_jaxpr/ppermute | solution.py:16
  524.5 15.7 %collective-permute-done = bf16[128,4608]{1,0:T(8,128)(2,1)S(1)} collective-permute-done((bf16[128,4608]{1,0:T(8,128)(2,1)}, bf16[128,4608]{1,0:T(8,128)(2,1)S(1)}, u32[]{:S(2)}, u32[]{:S(2)}) %collective-permute-start) | collective-permute-done | bytes 1179680 | tf_op jit(solution)/shard_map/while/body/eval_jaxpr/ppermute | solution.py:16
  554.0 15.9 %collective-permute-done = bf16[128,4608]{1,0:T(8,128)(2,1)S(1)} collective-permute-done((bf16[128,4608]{1,0:T(8,128)(2,1)}, bf16[128,4608]{1,0:T(8,128)(2,1)S(1)}, u32[]{:S(2)}, u32[]{:S(2)}) %collective-permute-start) | collective-permute-done | bytes 1179680 | tf_op jit(solution)/shard_map/while/body/eval_jaxpr/ppermute | solution.py:16
  571.8 17.1 %collective-permute-start.4 = (bf16[1,64,4608]{2,1,0:T(8,128)(2,1)}, bf16[1,64,4608]{2,1,0:T(8,128)(2,1)}, u32[]{:S(2)}, u32[]{:S(2)}) collective-permute-start(bf16[1,64,4608]{2,1,0:T(8,128)(2,1)} %slice.23), channel_id=1, source_target_pairs={{1,0},{2,1},{3,2},{4,3},{5,4},{6,5},{7,6},{8,7},{9,8},{10,9},{11,1... | collective-permute-start | bytes 1769480 | tf_op jit(solution)/shard_map/ppermute | solution.py:16
  605.5 3.9 collective-permute-done.1
  611.4 26.3 %psum.7 = f32[1,64]{1,0:T(1,128)S(1)} all-reduce(f32[1,64]{1,0:T(1,128)S(1)} %fusion.27), channel_id=1, replica_groups=mesh['section'=16,'dp'=16] {'dp'}, use_global_device_ids=true, to_apply=%region_8.9 | all-reduce | flops 64 | bytes 512 | tf_op jit(solution)/shard_map/psum | solution.py:138
  640.6 2.4 copy.19
  644.9 64.1 %reduce-scatter.4.cloned.1.call-done = bf16[288,256]{1,0:T(8,128)(2,1)} async-done(((bf16[4608,256]{1,0:T(8,128)(2,1)}), bf16[288,256]{1,0:T(8,128)(2,1)}) %reduce-scatter.4.cloned.1.call-update) | async-done | bytes 147472
  (358 shorter events, 244.4 us)
Async XLA Ops:
  7.2 701.8 %reduce-scatter.4.cloned.1.call-start = ((), (), s32[]{:S(2)}) async-start(), calls=%async_computation.1 | async-start | bytes 2506752
  20.3 27.5 %collective-permute-start = (bf16[128,4608]{1,0:T(8,128)(2,1)}, bf16[128,4608]{1,0:T(8,128)(2,1)S(1)}, u32[]{:S(2)}, u32[]{:S(2)}) collective-permute-start(bf16[128,4608]{1,0:T(8,128)(2,1)} %get-tuple-element.393), channel_id=1, source_target_pairs={{16,0},{32,16},{48,32},{64,48},{80,64},{96,80},{112,96},{128,112},... | collective-permute-start | bytes 3538952 | tf_op jit(solution)/shard_map/while/body/eval_jaxpr/ppermute | solution.py:16
  58.9 30.0 %collective-permute-start = (bf16[128,4608]{1,0:T(8,128)(2,1)}, bf16[128,4608]{1,0:T(8,128)(2,1)S(1)}, u32[]{:S(2)}, u32[]{:S(2)}) collective-permute-start(bf16[128,4608]{1,0:T(8,128)(2,1)} %get-tuple-element.393), channel_id=1, source_target_pairs={{16,0},{32,16},{48,32},{64,48},{80,64},{96,80},{112,96},{128,112},... | collective-permute-start | bytes 3538952 | tf_op jit(solution)/shard_map/while/body/eval_jaxpr/ppermute | solution.py:16
  100.0 27.1 %collective-permute-start = (bf16[128,4608]{1,0:T(8,128)(2,1)}, bf16[128,4608]{1,0:T(8,128)(2,1)S(1)}, u32[]{:S(2)}, u32[]{:S(2)}) collective-permute-start(bf16[128,4608]{1,0:T(8,128)(2,1)} %get-tuple-element.393), channel_id=1, source_target_pairs={{16,0},{32,16},{48,32},{64,48},{80,64},{96,80},{112,96},{128,112},... | collective-permute-start | bytes 3538952 | tf_op jit(solution)/shard_map/while/body/eval_jaxpr/ppermute | solution.py:16
  138.3 29.2 %collective-permute-start = (bf16[128,4608]{1,0:T(8,128)(2,1)}, bf16[128,4608]{1,0:T(8,128)(2,1)S(1)}, u32[]{:S(2)}, u32[]{:S(2)}) collective-permute-start(bf16[128,4608]{1,0:T(8,128)(2,1)} %get-tuple-element.393), channel_id=1, source_target_pairs={{16,0},{32,16},{48,32},{64,48},{80,64},{96,80},{112,96},{128,112},... | collective-permute-start | bytes 3538952 | tf_op jit(solution)/shard_map/while/body/eval_jaxpr/ppermute | solution.py:16
  178.6 27.3 %collective-permute-start = (bf16[128,4608]{1,0:T(8,128)(2,1)}, bf16[128,4608]{1,0:T(8,128)(2,1)S(1)}, u32[]{:S(2)}, u32[]{:S(2)}) collective-permute-start(bf16[128,4608]{1,0:T(8,128)(2,1)} %get-tuple-element.393), channel_id=1, source_target_pairs={{16,0},{32,16},{48,32},{64,48},{80,64},{96,80},{112,96},{128,112},... | collective-permute-start | bytes 3538952 | tf_op jit(solution)/shard_map/while/body/eval_jaxpr/ppermute | solution.py:16
  217.0 26.4 %collective-permute-start = (bf16[128,4608]{1,0:T(8,128)(2,1)}, bf16[128,4608]{1,0:T(8,128)(2,1)S(1)}, u32[]{:S(2)}, u32[]{:S(2)}) collective-permute-start(bf16[128,4608]{1,0:T(8,128)(2,1)} %get-tuple-element.393), channel_id=1, source_target_pairs={{16,0},{32,16},{48,32},{64,48},{80,64},{96,80},{112,96},{128,112},... | collective-permute-start | bytes 3538952 | tf_op jit(solution)/shard_map/while/body/eval_jaxpr/ppermute | solution.py:16
  254.6 25.5 %collective-permute-start = (bf16[128,4608]{1,0:T(8,128)(2,1)}, bf16[128,4608]{1,0:T(8,128)(2,1)S(1)}, u32[]{:S(2)}, u32[]{:S(2)}) collective-permute-start(bf16[128,4608]{1,0:T(8,128)(2,1)} %get-tuple-element.393), channel_id=1, source_target_pairs={{16,0},{32,16},{48,32},{64,48},{80,64},{96,80},{112,96},{128,112},... | collective-permute-start | bytes 3538952 | tf_op jit(solution)/shard_map/while/body/eval_jaxpr/ppermute | solution.py:16
  291.2 24.6 %collective-permute-start = (bf16[128,4608]{1,0:T(8,128)(2,1)}, bf16[128,4608]{1,0:T(8,128)(2,1)S(1)}, u32[]{:S(2)}, u32[]{:S(2)}) collective-permute-start(bf16[128,4608]{1,0:T(8,128)(2,1)} %get-tuple-element.393), channel_id=1, source_target_pairs={{16,0},{32,16},{48,32},{64,48},{80,64},{96,80},{112,96},{128,112},... | collective-permute-start | bytes 3538952 | tf_op jit(solution)/shard_map/while/body/eval_jaxpr/ppermute | solution.py:16
  326.9 23.6 %collective-permute-start = (bf16[128,4608]{1,0:T(8,128)(2,1)}, bf16[128,4608]{1,0:T(8,128)(2,1)S(1)}, u32[]{:S(2)}, u32[]{:S(2)}) collective-permute-start(bf16[128,4608]{1,0:T(8,128)(2,1)} %get-tuple-element.393), channel_id=1, source_target_pairs={{16,0},{32,16},{48,32},{64,48},{80,64},{96,80},{112,96},{128,112},... | collective-permute-start | bytes 3538952 | tf_op jit(solution)/shard_map/while/body/eval_jaxpr/ppermute | solution.py:16
  361.7 22.7 %collective-permute-start = (bf16[128,4608]{1,0:T(8,128)(2,1)}, bf16[128,4608]{1,0:T(8,128)(2,1)S(1)}, u32[]{:S(2)}, u32[]{:S(2)}) collective-permute-start(bf16[128,4608]{1,0:T(8,128)(2,1)} %get-tuple-element.393), channel_id=1, source_target_pairs={{16,0},{32,16},{48,32},{64,48},{80,64},{96,80},{112,96},{128,112},... | collective-permute-start | bytes 3538952 | tf_op jit(solution)/shard_map/while/body/eval_jaxpr/ppermute | solution.py:16
  395.6 21.8 %collective-permute-start = (bf16[128,4608]{1,0:T(8,128)(2,1)}, bf16[128,4608]{1,0:T(8,128)(2,1)S(1)}, u32[]{:S(2)}, u32[]{:S(2)}) collective-permute-start(bf16[128,4608]{1,0:T(8,128)(2,1)} %get-tuple-element.393), channel_id=1, source_target_pairs={{16,0},{32,16},{48,32},{64,48},{80,64},{96,80},{112,96},{128,112},... | collective-permute-start | bytes 3538952 | tf_op jit(solution)/shard_map/while/body/eval_jaxpr/ppermute | solution.py:16
  428.5 20.9 %collective-permute-start = (bf16[128,4608]{1,0:T(8,128)(2,1)}, bf16[128,4608]{1,0:T(8,128)(2,1)S(1)}, u32[]{:S(2)}, u32[]{:S(2)}) collective-permute-start(bf16[128,4608]{1,0:T(8,128)(2,1)} %get-tuple-element.393), channel_id=1, source_target_pairs={{16,0},{32,16},{48,32},{64,48},{80,64},{96,80},{112,96},{128,112},... | collective-permute-start | bytes 3538952 | tf_op jit(solution)/shard_map/while/body/eval_jaxpr/ppermute | solution.py:16
  460.5 19.9 %collective-permute-start = (bf16[128,4608]{1,0:T(8,128)(2,1)}, bf16[128,4608]{1,0:T(8,128)(2,1)S(1)}, u32[]{:S(2)}, u32[]{:S(2)}) collective-permute-start(bf16[128,4608]{1,0:T(8,128)(2,1)} %get-tuple-element.393), channel_id=1, source_target_pairs={{16,0},{32,16},{48,32},{64,48},{80,64},{96,80},{112,96},{128,112},... | collective-permute-start | bytes 3538952 | tf_op jit(solution)/shard_map/while/body/eval_jaxpr/ppermute | solution.py:16
  491.6 19.0 %collective-permute-start = (bf16[128,4608]{1,0:T(8,128)(2,1)}, bf16[128,4608]{1,0:T(8,128)(2,1)S(1)}, u32[]{:S(2)}, u32[]{:S(2)}) collective-permute-start(bf16[128,4608]{1,0:T(8,128)(2,1)} %get-tuple-element.393), channel_id=1, source_target_pairs={{16,0},{32,16},{48,32},{64,48},{80,64},{96,80},{112,96},{128,112},... | collective-permute-start | bytes 3538952 | tf_op jit(solution)/shard_map/while/body/eval_jaxpr/ppermute | solution.py:16
  521.8 18.4 %collective-permute-start = (bf16[128,4608]{1,0:T(8,128)(2,1)}, bf16[128,4608]{1,0:T(8,128)(2,1)S(1)}, u32[]{:S(2)}, u32[]{:S(2)}) collective-permute-start(bf16[128,4608]{1,0:T(8,128)(2,1)} %get-tuple-element.393), channel_id=1, source_target_pairs={{16,0},{32,16},{48,32},{64,48},{80,64},{96,80},{112,96},{128,112},... | collective-permute-start | bytes 3538952 | tf_op jit(solution)/shard_map/while/body/eval_jaxpr/ppermute | solution.py:16
  551.3 18.6 %collective-permute-start = (bf16[128,4608]{1,0:T(8,128)(2,1)}, bf16[128,4608]{1,0:T(8,128)(2,1)S(1)}, u32[]{:S(2)}, u32[]{:S(2)}) collective-permute-start(bf16[128,4608]{1,0:T(8,128)(2,1)} %get-tuple-element.393), channel_id=1, source_target_pairs={{16,0},{32,16},{48,32},{64,48},{80,64},{96,80},{112,96},{128,112},... | collective-permute-start | bytes 3538952 | tf_op jit(solution)/shard_map/while/body/eval_jaxpr/ppermute | solution.py:16
  571.0 19.7 %copy-start.5 = (bf16[4608,128]{1,0:T(8,128)(2,1)S(1)}, bf16[4608,128]{1,0:T(8,128)(2,1)}, u32[]{:S(2)}) copy-start(bf16[4608,128]{1,0:T(8,128)(2,1)} %get-tuple-element.444) | copy-start | bytes 3538948
  571.8 31.8 %collective-permute-start.4 = (bf16[1,64,4608]{2,1,0:T(8,128)(2,1)}, bf16[1,64,4608]{2,1,0:T(8,128)(2,1)}, u32[]{:S(2)}, u32[]{:S(2)}) collective-permute-start(bf16[1,64,4608]{2,1,0:T(8,128)(2,1)} %slice.23), channel_id=1, source_target_pairs={{1,0},{2,1},{3,2},{4,3},{5,4},{6,5},{7,6},{8,7},{9,8},{10,9},{11,1... | collective-permute-start | bytes 1769480 | tf_op jit(solution)/shard_map/ppermute | solution.py:16
  592.2 13.1 %collective-permute-start.3 = (bf16[1,64,128]{2,1,0:T(8,128)(2,1)}, bf16[1,64,128]{2,1,0:T(8,128)(2,1)S(1)}, u32[]{:S(2)}, u32[]{:S(2)}) collective-permute-start(bf16[1,64,128]{2,1,0:T(8,128)(2,1)} %slice.26), channel_id=1, source_target_pairs={{1,0},{2,1},{3,2},{4,3},{5,4},{6,5},{7,6},{8,7},{9,8},{10,9},{11,1... | collective-permute-start | bytes 49160 | tf_op jit(solution)/shard_map/ppermute | solution.py:16
  594.8 7.8 %collective-permute-start.2 = (bf16[1,64,128]{2,1,0:T(8,128)(2,1)}, bf16[1,64,128]{2,1,0:T(8,128)(2,1)}, u32[]{:S(2)}, u32[]{:S(2)}) collective-permute-start(bf16[1,64,128]{2,1,0:T(8,128)(2,1)} %slice.21), channel_id=1, source_target_pairs={{1,0},{2,1},{3,2},{4,3},{5,4},{6,5},{7,6},{8,7},{9,8},{10,9},{11,1... | collective-permute-start | bytes 49160 | tf_op jit(solution)/shard_map/ppermute | solution.py:16
  597.9 11.5 %collective-permute-start.1 = (bf16[1,64,4608]{2,1,0:T(8,128)(2,1)}, bf16[1,64,4608]{2,1,0:T(8,128)(2,1)}, u32[]{:S(2)}, u32[]{:S(2)}) collective-permute-start(bf16[1,64,4608]{2,1,0:T(8,128)(2,1)} %slice.25), channel_id=1, source_target_pairs={{1,0},{2,1},{3,2},{4,3},{5,4},{6,5},{7,6},{8,7},{9,8},{10,9},{11,1... | collective-permute-start | bytes 1769480 | tf_op jit(solution)/shard_map/ppermute | solution.py:16
  605.5 32.2 %copy-start.15 = (f32[1,1,64]{2,1,0:T(1,128)S(1)}, f32[1,1,64]{2,1,0:T(1,128)}, u32[]{:S(2)}) copy-start(f32[1,1,64]{2,1,0:T(1,128)} %param.15) | copy-start | bytes 772
  605.5 32.9 %copy-start.14 = (f32[128]{0:T(128)S(1)}, f32[128]{0:T(128)}, u32[]{:S(2)}) copy-start(f32[128]{0:T(128)} %copy-done.12) | copy-start | bytes 1540
  (75 other events, 141.2 us)
Sparse Core Ops, SparseCore 0:
  643.2 65.7 reduce-scatter.3
where the time goes:
time: 724 us; the launch traced here: 718 us
  waiting for transfers between devices  408 us (56%)
  other arithmetic  124 us (17%)
  matrix products  57.6 us (8%)
  local copies, waits for them, and re-layouts  43.9 us (6%)
  starting transfers between devices  43.4 us (6%)
  blocking collectives  26.3 us (4%)
  between operations  14.3 us (2%)
    ppermute x20, waiting for transfers between devices, passed_along(): lax.ppermute(value, axis, [(source, source + steps) for source in range(l...  344 us
    unnamed x2, waiting for transfers between devices  64.1 us
    ppermute x20, starting transfers between devices, passed_along(): lax.ppermute(value, axis, [(source, source + steps) for source in range(l...  43.3 us
    broadcast_in_dim x16, other arithmetic, chain_tick(): lax.dynamic_update_index_in_dim(arrived, jnp.where(is_valid, incoming_gra...  37.2 us
    while x128, local copies, waits for them, and re-layouts  32.5 us
    broadcast_in_dim x16, other arithmetic, chain_tick(): lax.dynamic_update_index_in_dim(outgoing_gradient, jnp.where(is_valid, fi...  31.9 us
    dot_general x16, matrix products, section_back(): lax.dot_general(low_rank, down_matrix, (((1,), (1,)), ((), ())), preferre...  31.6 us
    psum x1, blocking collectives, on_device(): pair_sum = lax.psum(partial_sums, 'dp')  26.3 us
  transfers between devices with their start and end apart: 21, of which 18 were waited for; matrix products, arithmetic and copies ran while one was open for 5% of the time, Pallas kernels for 0%

commit v1 on v0

v1 whole, which is shorter than its diff:
```python
import functools

import jax
import jax.numpy as jnp
from jax import lax
from jax.experimental import pallas as pl
from jax.experimental.pallas import tpu as pltpu
from jax.sharding import PartitionSpec as P

OWN = 8
NORM_EPS = 1e-06
MESH = pl.DeviceIdType.MESH
F32, BF16 = jnp.float32, jnp.bfloat16
R = 8
G = 16
LANE = 128
CHUNKS = 3


def dot(a, b):
    return jnp.dot(a, b, preferred_element_type=F32)


def dot_nt(a, b):
    return lax.dot_general(a, b, (((1,), (1,)), ((), ())), preferred_element_type=F32)


def halves(v, half):
    return jnp.concatenate([v[:, :half], v[:, half:]], axis=0)


def kernel(n_sec, n_dp, *refs):
    (acts, og, gains, dn, up, thr, lens, own, ig, lora, owned,
     xv, flat, ucat, dv, dtc, normed, xp, arr, outp, outf, scale, hidf, hidb, lowf, lowb,
     r_n, r_a, r_l, r_h, nw, hw, parts, part_f, other, lora_v, hid_t, low_t, doc_row, doc_col,
     s_load, s_out, s_chain, c_send, rs, rso, ss, sso, p_send, p_recv, o_send, o_recv) = refs
    tok, feat = xv.shape
    half = feat // 2
    n_docs = lens.shape[1]
    pieces, groups = tok // R, tok // G
    n_z = n_dp // 2
    per_chip = feat // n_z
    win = r_n.shape[1]
    blocks = n_dp // 2
    span = blocks * tok
    cols = tok + tok // 2
    lanes = half // CHUNKS

    sec = lax.axis_index("section")
    me = lax.axis_index("dp")
    z, core = me // 2, lax.rem(me, 2)
    side = me // blocks
    slot = lax.rem(me, blocks)
    last = n_sec - 1
    first_half = core == 0

    def load(src, dst, i):
        return pltpu.make_async_copy(src, dst, s_load.at[i])

    loads = [
        load(acts, xv, 0),
        load(dn, dv, 1),
        load(up.at[pl.ds(0, half)], ucat.at[:, pl.ds(0, LANE)], 2),
        load(up.at[pl.ds(half, half)], ucat.at[:, pl.ds(LANE, LANE)], 3),
    ]
    for c in loads:
        c.start()

    @pl.when(sec == last)
    def _():
        load(og, flat, 4).start()

    barrier = pltpu.get_barrier_semaphore()

    def greet(who):
        pl.semaphore_signal(barrier, inc=1, device_id=who, device_id_type=MESH)

    @pl.when(sec > 0)
    def _():
        greet({"section": sec - 1})

    @pl.when(sec < last)
    def _():
        greet({"section": sec + 1})

    for peer in range(n_dp):
        @pl.when(me != peer)
        def _():
            greet({"dp": peer})

    @pl.when(core == 1)
    def _():
        for r in (r_n, r_a, r_l, r_h):
            r[pl.ds(span, tok // 2), :] = jnp.zeros((tok // 2, r.shape[1]), BF16)

    loads[0].wait()

    def norm_group(q, _):
        rows = pl.ds(pl.multiple_of(q * G, G), G)
        v = xv[rows, :].astype(F32)
        s = lax.rsqrt(jnp.sum(v * v, axis=1, keepdims=True) / feat + NORM_EPS)
        scale[rows, :] = jnp.broadcast_to(s, (G, LANE))
        normed[rows, :] = (v * s * gains[...]).astype(BF16)
        xp[2 * q] = halves(v[:R], half).astype(BF16)
        xp[2 * q + 1] = halves(v[R:], half).astype(BF16)
        return 0

    lax.fori_loop(0, groups, norm_group, 0)
    loads[1].wait()
    hidf[...] = jnp.zeros_like(hidf)

    def down_tile(t, _):
        here = pl.ds(pl.multiple_of(t * LANE, LANE), LANE)
        there = pl.ds(pl.multiple_of(t * LANE + half, LANE), LANE)
        dtc[pl.ds(0, LANE), here] = (dv[here, :].astype(F32).T * gains[:, here]).astype(BF16)
        dtc[pl.ds(LANE, LANE), here] = (dv[there, :].astype(F32).T * gains[:, there]).astype(BF16)
        hidf[...] += dot(normed[:, here], dv[here, :]) + dot(normed[:, there], dv[there, :])
        return 0

    lax.fori_loop(0, half // LANE, down_tile, 0)
    hidb[...] = hidf[...].astype(BF16)

    @pl.when(sec == last)
    def _():
        load(og, flat, 4).wait()

        def pack(q, _):
            rows = pl.ds(pl.multiple_of(q * G, G), G)
            v = flat[rows, :].astype(F32)
            arr[2 * q] = halves(v[:R], half).astype(BF16)
            arr[2 * q + 1] = halves(v[R:], half).astype(BF16)
            return 0

        lax.fori_loop(0, groups, pack, 0)

    loads[2].wait()
    loads[3].wait()

    ends = jnp.where(sec > 0, 1, 0) + jnp.where(sec < last, 1, 0)
    pl.semaphore_wait(barrier, n_dp - 1 + ends)

    def spread(src, dst, i, row, n, window):
        for zz in range(n_z):
            start = per_chip * zz // LANE * LANE if window else 0
            width = win if window else LANE
            s = src.at[pl.ds(row, n), pl.ds(start, width)]

            def to(dest_core, at, send, recv):
                d = dst.at[pl.ds(at, n), :]
                dest = 2 * zz + dest_core

                @pl.when(dest == me)
                def _():
                    pltpu.make_async_copy(s, d, recv.at[i]).start()

                @pl.when(dest != me)
                def _():
                    pltpu.make_async_remote_copy(
                        src_ref=s, dst_ref=d, send_sem=send.at[i], recv_sem=recv.at[i],
                        device_id={"dp": dest}, device_id_type=MESH,
                    ).start()

            to(side, pl.multiple_of(slot * tok + row, G), ss, rs)

            @pl.when((me == blocks) & (row < tok // 2))
            def _():
                to(0, pl.multiple_of(span + lax.rem(row, tok // 2), G), sso, rso)

    def spread_own():
        def group(q, _):
            row = pl.multiple_of(q * G, G)
            spread(normed, r_n, 0, row, G, True)
            spread(hidb, r_h, 1, row, G, False)
            return 0

        lax.fori_loop(0, groups, group, 0)

    def doc_tables():
        k_row = lax.broadcasted_iota(jnp.int32, (n_docs, n_docs), 1)
        k_col = lax.broadcasted_iota(jnp.int32, (n_docs, n_docs), 0)
        len_row = lens[...].astype(F32)
        len_col = jnp.sum(jnp.where(k_row == k_col, len_row, 0.0), axis=1, keepdims=True)
        ends_col = jnp.sum(jnp.where(k_row <= k_col, len_row, 0.0), axis=1, keepdims=True)
        ends_row = jnp.sum(jnp.where(k_col <= k_row, len_col, 0.0), axis=0, keepdims=True)
        base = core * span

        def at(b, _):
            start = pl.multiple_of(b * tok, tok)
            pos_r = (lax.broadcasted_iota(jnp.int32, (n_docs, tok), 1) + (base + start)).astype(F32)
            doc_row[:, pl.ds(start, tok)] = jnp.broadcast_to(
                jnp.sum(jnp.where(ends_col <= pos_r, 1.0, 0.0), axis=0, keepdims=True), (8, tok))
            pos_c = (lax.broadcasted_iota(jnp.int32, (tok, n_docs), 0) + (base + start)).astype(F32)
            doc_col[pl.ds(start, tok), :] = jnp.broadcast_to(
                jnp.sum(jnp.where(ends_row <= pos_c, 1.0, 0.0), axis=1, keepdims=True), (tok, LANE))
            return 0

        lax.fori_loop(0, blocks + 1, at, 0)

    @pl.when(sec < n_sec // 2)
    def _():
        spread_own()

    def chain_copy(p, c):
        there = pl.ds(c * lanes, lanes)
        return pltpu.make_async_remote_copy(
            src_ref=outp.at[p, :, there], dst_ref=arr.at[p, :, there],
            send_sem=c_send, recv_sem=s_chain.at[p, c],
            device_id={"section": jnp.maximum(sec - 1, 0)}, device_id_type=MESH,
        )

    def piece(p):
        row = pl.multiple_of(p * R, R)
        rows = pl.ds(row, R)
        for c in range(CHUNKS):
            @pl.when(sec < last)
            def _():
                chain_copy(p, c).wait_recv()

        both = dot(arr[p], ucat[...])
        low = (both[:R, :LANE] + both[R:, LANE:]).astype(BF16).astype(F32)
        lowf[rows, :] = low
        s = scale[rows, :1]
        k = s * s * (jnp.sum(low * hidf[rows, :], axis=1, keepdims=True) / feat)
        zero = jnp.zeros_like(low)
        wide = jnp.concatenate(
            [jnp.concatenate([low, zero], axis=1), jnp.concatenate([zero, low], axis=1)], axis=0
        ).astype(BF16)
        s2, k2 = jnp.concatenate([s, s], axis=0), jnp.concatenate([k, k], axis=0)
        for c in range(CHUNKS):
            there = pl.ds(c * lanes, lanes)
            back = dot(wide, dtc[:, there])
            out = arr[p, :, there].astype(F32) + s2 * back - k2 * xp[p, :, there].astype(F32)
            outp[p, :, there] = out.astype(BF16)

            @pl.when(sec > 0)
            def _():
                chain_copy(p, c).start()

    def group(q, _):
        piece(2 * q)
        piece(2 * q + 1)
        row = pl.multiple_of(q * G, G)
        rows = pl.ds(row, G)

        def unpack(src):
            a, b = src[2 * q].astype(F32), src[2 * q + 1].astype(F32)
            return (jnp.concatenate([a[:R], b[:R]], axis=0).astype(BF16),
                    jnp.concatenate([a[R:], b[R:]], axis=0).astype(BF16))

        @pl.when(sec < last)
        def _():
            lo, hi = unpack(arr)
            flat[rows, pl.ds(0, half)] = lo
            flat[rows, pl.ds(half, half)] = hi

        lo, hi = unpack(outp)
        outf[rows, pl.ds(0, half)] = lo
        outf[rows, pl.ds(half, half)] = hi
        lowb[rows, :] = lowf[rows, :].astype(BF16)
        spread(flat, r_a, 2, row, G, True)
        spread(lowb, r_l, 3, row, G, False)
        pltpu.make_async_copy(outf.at[rows], ig.at[rows], s_out.at[0]).start()
        return 0

    lax.fori_loop(0, groups, group, 0)

    @pl.when(sec >= n_sec // 2)
    def _():
        spread_own()

    def arrived(dst, i):
        pltpu.make_async_copy(dst.at[pl.ds(0, span)], dst.at[pl.ds(0, span)], rs.at[i]).wait()

        @pl.when(first_half)
        def _():
            over = dst.at[pl.ds(span, tok // 2)]
            pltpu.make_async_copy(over, over, rso.at[i]).wait()

    doc_tables()
    arrived(r_n, 0)
    arrived(r_h, 1)
    offset = lax.rem(z, 2) * (LANE // 2)
    lane = lax.broadcasted_iota(jnp.int32, (1, win), 1)
    inside = jnp.where((lane >= offset) & (lane < offset + per_chip), 1.0, 0.0)
    column = jnp.where(lax.broadcasted_iota(jnp.int32, (1, cols), 1) < tok, 1.0, 2.0)

    def mine(src, b):
        return (src[pl.ds(b * tok, tok), :].astype(F32) * inside).astype(BF16)

    for b in range(blocks):
        there = pl.ds(b * tok, cols)
        same = doc_col[pl.ds(b * tok, tok), :1] == doc_row[:1, there]
        weight = jnp.where(same, column, 0.0)
        nw[b] = weight * dot_nt(mine(r_n, b), r_n[there, :])
        hw[b] = weight * dot_nt(r_h[pl.ds(b * tok, tok), :], r_h[there, :])
        hid_t[:, pl.ds(b * tok, tok)] = r_h[pl.ds(b * tok, tok), :].astype(F32).T

    arrived(r_l, 3)
    arrived(r_a, 2)
    total = jnp.zeros((1, LANE), F32)
    doc_lane = lax.broadcasted_iota(jnp.int32, (tok, LANE), 1).astype(F32)
    for b in range(blocks):
        there, here = pl.ds(b * tok, cols), pl.ds(b * tok, tok)
        pair = nw[b] * dot_nt(r_l[here, :], r_l[there, :]) + hw[b] * dot_nt(mine(r_a, b), r_a[there, :])
        row_sum = jnp.sum(pair, axis=1, keepdims=True)
        total += jnp.sum(jnp.where(doc_col[here, :] == doc_lane, row_sum, 0.0), axis=0, keepdims=True)
    parts[me] = jnp.broadcast_to(total, (8, LANE))

    for peer in range(n_dp):
        @pl.when(me != peer)
        def _():
            pltpu.make_async_remote_copy(
                src_ref=parts.at[me], dst_ref=parts.at[me], send_sem=p_send, recv_sem=p_recv,
                device_id={"dp": peer}, device_id_type=MESH,
            ).start()

    for b in range(blocks):
        here = pl.ds(b * tok, tok)
        low_t[:, here] = r_l[here, :].astype(F32).T

    most = parts.at[pl.ds(0, n_dp - 1)]
    pltpu.make_async_copy(most, most, p_recv).wait()
    pair_sum = jnp.sum(parts[...], axis=0)[:1, :n_docs]
    ratio = jnp.sqrt(pair_sum / (feat * LANE) + NORM_EPS) / thr[...]
    clip = jnp.minimum(1.0, 1.0 / ratio)
    k_row = lax.broadcasted_iota(jnp.int32, (n_docs, n_docs), 1)
    k_col = lax.broadcasted_iota(jnp.int32, (n_docs, n_docs), 0)
    clip_col = jnp.sum(jnp.where(k_row == k_col, clip, 0.0), axis=1, keepdims=True)
    doc_id = lax.broadcasted_iota(jnp.int32, (n_docs, span), 0).astype(F32)
    token_clip = jnp.sum(
        jnp.where(doc_row[:1, pl.ds(0, span)] == doc_id, clip_col, 0.0), axis=0, keepdims=True)
    down = dot((low_t[...] * token_clip).astype(BF16), r_n[pl.ds(0, span), :])
    up_g = dot((hid_t[...] * token_clip).astype(BF16), r_a[pl.ds(0, span), :])
    part_f[:, pl.ds(0, LANE)] = down.T
    part_f[:, pl.ds(LANE, LANE)] = up_g.T
    own_rows = pl.multiple_of(offset + core * (per_chip // 2), 8)
    far_rows = pl.multiple_of(offset + (1 - core) * (per_chip // 2), 8)
    swap = pltpu.make_async_remote_copy(
        src_ref=part_f.at[pl.ds(far_rows, per_chip // 2)], dst_ref=other,
        send_sem=o_send, recv_sem=o_recv,
        device_id={"dp": 2 * z + (1 - core)}, device_id_type=MESH,
    )
    swap.start()

    own_row = jnp.where(own[...] == me, 1.0, 0.0)
    own_col = jnp.sum(jnp.where(k_row == k_col, own_row, 0.0), axis=1, keepdims=True)
    rank_col = jnp.sum(jnp.where(k_row <= k_col, own_row, 0.0), axis=1, keepdims=True) - 1.0
    ratio_col = jnp.sum(jnp.where(k_row == k_col, ratio, 0.0), axis=1, keepdims=True)
    slot_id = lax.broadcasted_iota(jnp.int32, (n_docs, OWN), 1).astype(F32)
    held = jnp.where((own_col > 0.5) & (rank_col == slot_id), ratio_col, 0.0)
    owned[...] = jnp.sum(held, axis=0, keepdims=True)

    swap.wait()
    lora_v[...] = (part_f[pl.ds(own_rows, per_chip // 2), :] + other[...]) / n_docs
    store = pltpu.make_async_copy(lora_v, lora, s_out.at[1])
    store.start()

    pltpu.make_async_copy(most, most, p_send).wait()

    @pl.when(sec > 0)
    def _():
        pltpu.make_async_copy(outp, outp, c_send).wait()

    for i, dst in enumerate((r_n, r_h, r_a, r_l)):
        @pl.when(core == side)
        def _():
            whole = dst.at[pl.ds(0, (n_z - 1) * tok)]
            pltpu.make_async_copy(whole, whole, ss.at[i]).wait()

        @pl.when(core != side)
        def _():
            whole = dst.at[pl.ds(0, n_z * tok)]
            pltpu.make_async_copy(whole, whole, ss.at[i]).wait()

        @pl.when(me == blocks)
        def _():
            whole = dst.at[pl.ds(0, (n_z - 1) * (tok // 2))]
            pltpu.make_async_copy(whole, whole, sso.at[i]).wait()

    pltpu.make_async_copy(outf, outf, s_out.at[0]).wait()
    store.wait()


def solution(mesh):
    n_sec, n_dp = mesh.shape["section"], mesh.shape["dp"]
    n_z = n_dp // 2

    def on_device(acts, output_gradient, gains, down, up, thresholds, lengths, owners):
        tok, feat = acts.shape[2:]
        rank = down.shape[2]
        half = feat // 2
        per_chip = feat // n_z
        win = -(-per_chip // LANE) * LANE
        pieces, blocks = tok // R, n_dp // 2
        span = blocks * tok
        long = span + tok // 2
        cols = tok + tok // 2
        hbm = pl.BlockSpec(memory_space=pl.ANY)
        vmem = pl.BlockSpec(memory_space=pltpu.VMEM)
        dma = pltpu.SemaphoreType.DMA
        packed = pltpu.VMEM((pieces, 2 * R, half), BF16)
        whole = pltpu.VMEM((tok, feat), BF16)
        ig, lora, owned = pl.pallas_call(
            functools.partial(kernel, n_sec, n_dp),
            out_shape=(
                jax.ShapeDtypeStruct((tok, feat), BF16),
                jax.ShapeDtypeStruct((feat // n_dp, 2 * rank), F32),
                jax.ShapeDtypeStruct((1, OWN), F32),
            ),
            in_specs=[hbm, hbm, vmem, hbm, hbm, vmem, vmem, vmem],
            out_specs=(hbm, hbm, vmem),
            scratch_shapes=[
                whole,
                whole,
                pltpu.VMEM((half, 2 * rank), BF16),
                pltpu.VMEM((feat, rank), BF16),
                pltpu.VMEM((2 * rank, half), BF16),
                whole,
                packed,
                packed,
                packed,
                whole,
                pltpu.VMEM((tok, LANE), F32),
                pltpu.VMEM((tok, rank), F32),
                pltpu.VMEM((tok, rank), BF16),
                pltpu.VMEM((tok, rank), F32),
                pltpu.VMEM((tok, rank), BF16),
                pltpu.VMEM((long, win), BF16),
                pltpu.VMEM((long, win), BF16),
                pltpu.VMEM((long, rank), BF16),
                pltpu.VMEM((long, rank), BF16),
                pltpu.VMEM((blocks, tok, cols), F32),
                pltpu.VMEM((blocks, tok, cols), F32),
                pltpu.VMEM((n_dp, 8, LANE), F32),
                pltpu.VMEM((win, 2 * rank), F32),
                pltpu.VMEM((per_chip // 2, 2 * rank), F32),
                pltpu.VMEM((per_chip // 2, 2 * rank), F32),
                pltpu.VMEM((rank, span), F32),
                pltpu.VMEM((rank, span), F32),
                pltpu.VMEM((8, span + tok), F32),
                pltpu.VMEM((span + tok, LANE), F32),
                dma((5,)),
                dma((2,)),
                dma((pieces, CHUNKS)),
                dma,
                dma((4,)),
                dma((4,)),
                dma((4,)),
                dma((4,)),
                dma,
                dma,
                dma,
                dma,
            ],
            compiler_params=pltpu.CompilerParams(
                collective_id=0, has_side_effects=True, vmem_limit_bytes=56 << 20
            ),
        )(acts[0, 0], output_gradient[0], gains, down[0], up[0], thresholds[0], lengths, owners)
        return ig[None, None], lora[None], owned[None]

    placed = (
        P("section", None, "dp", None),
        P(None, "dp", None),
        P("section", None),
        P("section", None, None),
        P("section", None, None),
        P("section", None, None),
        P(),
        P(),
    )
    return jax.shard_map(
        on_device,
        mesh=mesh,
        in_specs=placed,
        out_specs=(P("section", None, "dp", None), P("section", "dp", None), P("section", None, "dp")),
        check_vma=False,
    )
```

time: 724 us -> 136 us (0.19)
  the two profiles are of different devices: /device:TPU:1 before, /device:TPU:17 now
where the time goes in v1:
time: 136 us
  Pallas kernels  131 us (96%)
  local copies, waits for them, and re-layouts  3.63 us (3%)
    pallas_call x1, Pallas kernels, on_device(): pl.pallas_call(functools.partial(kernel, n_sec, n_dp), out_shape=(jax.Sha...  131 us
    unnamed x7, local copies, waits for them, and re-layouts  3.63 us

profile of v1, /device:TPU:17, one launch (start us, length us, event | category | flops | bytes accessed | tf_op | source)
XLA Modules:
  0.0 135.7 jit_solution(2660315821142859180)
XLA Ops:
  0.6 131.4 %shard_map.103 = (bf16[128,4608]{1,0:T(8,128)(2,1)}, f32[288,256]{1,0:T(8,128)}, f32[1,8]{1,0:T(1,128)}) custom-call(bf16[128,4608]{1,0:T(8,128)(2,1)} %bitcast.8, bf16[128,4608]{1,0:T(8,128)(2,1)} %bitcast.9, f32[1,4608]{1,0:T(1,128)} %refs_2_.1, bf16[4608,128]{1,0:T(8,128)(2,1)} %bitcast.10, bf16[4608,128]{1,0:T(8,128)(2,1)} %bitcast.11, ...), custom_call_target="tpu_custom_call" | custom-call | tf_op jit(solution)/shard_map/pallas_call | solution.py:403
  132.0 0.0 copy-start
  132.0 0.0 copy-start.1
  132.1 2.4 %copy.14 = bf16[1,1,128,4608]{3,2,1,0:T(8,128)(2,1)} copy(bf16[1,1,128,4608]{3,2,1,0:T(8,128)(2,1)} %bitcast.12) | data formatting | bytes 2359296
  134.5 0.0 copy-done
  134.5 0.7 copy.15
  135.2 0.0 copy-done.1
  135.2 0.5 copy.16
Async XLA Ops:
  132.0 2.4 %copy-start = (f32[288,256]{1,0:T(8,128)S(1)}, f32[288,256]{1,0:T(8,128)}, u32[]{:S(2)}) copy-start(f32[288,256]{1,0:T(8,128)} %get-tuple-element.7) | copy-start | bytes 884740
  132.0 3.1 %copy-start.1 = (f32[1,8]{1,0:T(1,128)S(1)}, f32[1,8]{1,0:T(1,128)}, u32[]{:S(2)}) copy-start(f32[1,8]{1,0:T(1,128)} %get-tuple-element.8) | copy-start | bytes 100

commit v2 on v1

--- a/solution.py
+++ b/solution.py
@@ -15,6 +15,7 @@
 G = 16
 LANE = 128
 CHUNKS = 3
+LATE = 2
 
 
 def dot(a, b):
@@ -31,8 +32,8 @@
 
 def kernel(n_sec, n_dp, *refs):
     (acts, og, gains, dn, up, thr, lens, own, ig, lora, owned,
-     xv, flat, ucat, dv, dtc, normed, xp, arr, outp, outf, scale, hidf, hidb, lowf, lowb,
-     r_n, r_a, r_l, r_h, nw, hw, parts, part_f, other, lora_v, hid_t, low_t, doc_row, doc_col,
+     xv, flat, ucat, dv, dtc, normed, xp, arr, outp, outf, scale, hidf, hidb, lowf, stage,
+     r_n, r_a, r_h, nw, hw, parts, part_f, other, lora_v, hid_t, low_t, doc_row, doc_col,
      s_load, s_out, s_chain, c_send, rs, rso, ss, sso, p_send, p_recv, o_send, o_recv) = refs
     tok, feat = xv.shape
     half = feat // 2
@@ -90,7 +91,7 @@
 
     @pl.when(core == 1)
     def _():
-        for r in (r_n, r_a, r_l, r_h):
+        for r in (r_n, r_a, r_h):
             r[pl.ds(span, tok // 2), :] = jnp.zeros((tok // 2, r.shape[1]), BF16)
 
     loads[0].wait()
@@ -139,41 +140,62 @@
     ends = jnp.where(sec > 0, 1, 0) + jnp.where(sec < last, 1, 0)
     pl.semaphore_wait(barrier, n_dp - 1 + ends)
 
-    def spread(src, dst, i, row, n, window):
+    def send(src, dst, i, zz, dest_core, row, n, sems):
+        at = pl.multiple_of(row, G)
+        d = dst.at[pl.ds(at, n), :]
+        dest = 2 * zz + dest_core
+
+        @pl.when(dest == me)
+        def _():
+            pltpu.make_async_copy(src, d, sems[1].at[i]).start()
+
+        @pl.when(dest != me)
+        def _():
+            pltpu.make_async_remote_copy(
+                src_ref=src, dst_ref=d, send_sem=sems[0].at[i], recv_sem=sems[1].at[i],
+                device_id={"dp": dest}, device_id_type=MESH,
+            ).start()
+
+    def spread_own(zz):
+        start = pl.multiple_of(per_chip * zz // LANE * LANE, LANE)
+        there = pl.ds(start, win)
+        send(normed.at[:, there], r_n, 0, zz, side, slot * tok, tok, (ss, rs))
+        send(hidb, r_h, 1, zz, side, slot * tok, tok, (ss, rs))
+
+        @pl.when(me == blocks)
+        def _():
+            top = pl.ds(0, tok // 2)
+            send(normed.at[top, there], r_n, 0, zz, 0, span, tok // 2, (sso, rso))
+            send(hidb.at[top], r_h, 1, zz, 0, span, tok // 2, (sso, rso))
+
+    def spread_all(zz, _):
+        spread_own(zz)
+        return 0
+
+    def spread_arriving(q):
+        row = q * G
+        a, b = arr[2 * q].astype(F32), arr[2 * q + 1].astype(F32)
+        low = lowf[pl.ds(pl.multiple_of(row, G), G), :].astype(BF16)
+        lane = lax.broadcasted_iota(jnp.int32, (1, LANE), 1)
         for zz in range(n_z):
-            start = per_chip * zz // LANE * LANE if window else 0
-            width = win if window else LANE
-            s = src.at[pl.ds(row, n), pl.ds(start, width)]
-
-            def to(dest_core, at, send, recv):
-                d = dst.at[pl.ds(at, n), :]
-                dest = 2 * zz + dest_core
-
-                @pl.when(dest == me)
-                def _():
-                    pltpu.make_async_copy(s, d, recv.at[i]).start()
-
-                @pl.when(dest != me)
-                def _():
-                    pltpu.make_async_remote_copy(
-                        src_ref=s, dst_ref=d, send_sem=send.at[i], recv_sem=recv.at[i],
-                        device_id={"dp": dest}, device_id_type=MESH,
-                    ).start()
-
-            to(side, pl.multiple_of(slot * tok + row, G), ss, rs)
+            first = per_chip * zz
+            start = first // LANE * LANE
+            part = start // half
+            r0, l0 = part * R, start - part * half
+            w = jnp.concatenate([a[r0:r0 + R, l0:l0 + win], b[r0:r0 + R, l0:l0 + win]], axis=0)
+            w = jnp.concatenate([
+                w[:, :LANE] * jnp.where(lane >= first - start, 1.0, 0.0),
+                w[:, LANE:win - LANE],
+                w[:, win - LANE:] * jnp.where(lane < first + per_chip - (start + win - LANE), 1.0, 0.0),
+            ], axis=1)
+            stage[q, zz, :, pl.ds(0, win)] = w.astype(BF16)
+            stage[q, zz, :, pl.ds(win, LANE)] = low
+        for zz in range(n_z):
+            send(stage.at[q, zz], r_a, 2, zz, side, slot * tok + row, G, (ss, rs))
 
             @pl.when((me == blocks) & (row < tok // 2))
             def _():
-                to(0, pl.multiple_of(span + lax.rem(row, tok // 2), G), sso, rso)
-
-    def spread_own():
-        def group(q, _):
-            row = pl.multiple_of(q * G, G)
-            spread(normed, r_n, 0, row, G, True)
-            spread(hidb, r_h, 1, row, G, False)
-            return 0
-
-        lax.fori_loop(0, groups, group, 0)
+                send(stage.at[q, zz], r_a, 2, zz, 0, span + lax.rem(row, tok // 2), G, (sso, rso))
 
     def doc_tables():
         k_row = lax.broadcasted_iota(jnp.int32, (n_docs, n_docs), 1)
@@ -196,9 +218,11 @@
 
         lax.fori_loop(0, blocks + 1, at, 0)
 
-    @pl.when(sec < n_sec // 2)
-    def _():
-        spread_own()
+    early = sec < n_sec - LATE
+
+    @pl.when(early)
+    def _():
+        lax.fori_loop(0, n_z, spread_all, 0)
 
     def chain_copy(p, c):
         there = pl.ds(c * lanes, lanes)
@@ -211,12 +235,14 @@
     def piece(p):
         row = pl.multiple_of(p * R, R)
         rows = pl.ds(row, R)
+        both = jnp.zeros((2 * R, 2 * LANE), F32)
         for c in range(CHUNKS):
             @pl.when(sec < last)
             def _():
                 chain_copy(p, c).wait_recv()
 
-        both = dot(arr[p], ucat[...])
+            there = pl.ds(c * lanes, lanes)
+            both += dot(arr[p, :, there], ucat[there, :])
         low = (both[:R, :LANE] + both[R:, LANE:]).astype(BF16).astype(F32)
         lowf[rows, :] = low
         s = scale[rows, :1]
@@ -247,26 +273,19 @@
             return (jnp.concatenate([a[:R], b[:R]], axis=0).astype(BF16),
                     jnp.concatenate([a[R:], b[R:]], axis=0).astype(BF16))
 
-        @pl.when(sec < last)
-        def _():
-            lo, hi = unpack(arr)
-            flat[rows, pl.ds(0, half)] = lo
-            flat[rows, pl.ds(half, half)] = hi
-
         lo, hi = unpack(outp)
         outf[rows, pl.ds(0, half)] = lo
         outf[rows, pl.ds(half, half)] = hi
-        lowb[rows, :] = lowf[rows, :].astype(BF16)
-        spread(flat, r_a, 2, row, G, True)
-        spread(lowb, r_l, 3, row, G, False)
+        spread_arriving(q)
+
+        @pl.when(jnp.logical_not(early))
+        def _():
+            spread_own(q)
+
         pltpu.make_async_copy(outf.at[rows], ig.at[rows], s_out.at[0]).start()
         return 0
 
     lax.fori_loop(0, groups, group, 0)
-
-    @pl.when(sec >= n_sec // 2)
-    def _():
-        spread_own()
 
     def arrived(dst, i):
         pltpu.make_async_copy(dst.at[pl.ds(0, span)], dst.at[pl.ds(0, span)], rs.at[i]).wait()
@@ -295,13 +314,13 @@
         hw[b] = weight * dot_nt(r_h[pl.ds(b * tok, tok), :], r_h[there, :])
         hid_t[:, pl.ds(b * tok, tok)] = r_h[pl.ds(b * tok, tok), :].astype(F32).T
 
-    arrived(r_l, 3)
     arrived(r_a, 2)
+    win_l, low_l = pl.ds(0, win), pl.ds(win, LANE)
     total = jnp.zeros((1, LANE), F32)
     doc_lane = lax.broadcasted_iota(jnp.int32, (tok, LANE), 1).astype(F32)
     for b in range(blocks):
         there, here = pl.ds(b * tok, cols), pl.ds(b * tok, tok)
-        pair = nw[b] * dot_nt(r_l[here, :], r_l[there, :]) + hw[b] * dot_nt(mine(r_a, b), r_a[there, :])
+        pair = nw[b] * dot_nt(r_a[here, low_l], r_a[there, low_l]) + hw[b] * dot_nt(r_a[here, win_l], r_a[there, win_l])
         row_sum = jnp.sum(pair, axis=1, keepdims=True)
         total += jnp.sum(jnp.where(doc_col[here, :] == doc_lane, row_sum, 0.0), axis=0, keepdims=True)
     parts[me] = jnp.broadcast_to(total, (8, LANE))
@@ -316,7 +335,7 @@
 
     for b in range(blocks):
         here = pl.ds(b * tok, tok)
-        low_t[:, here] = r_l[here, :].astype(F32).T
+        low_t[:, here] = r_a[here, low_l].astype(F32).T
 
     most = parts.at[pl.ds(0, n_dp - 1)]
     pltpu.make_async_copy(most, most, p_recv).wait()
@@ -330,7 +349,7 @@
     token_clip = jnp.sum(
         jnp.where(doc_row[:1, pl.ds(0, span)] == doc_id, clip_col, 0.0), axis=0, keepdims=True)
     down = dot((low_t[...] * token_clip).astype(BF16), r_n[pl.ds(0, span), :])
-    up_g = dot((hid_t[...] * token_clip).astype(BF16), r_a[pl.ds(0, span), :])
+    up_g = dot((hid_t[...] * token_clip).astype(BF16), r_a[pl.ds(0, span), win_l])
     part_f[:, pl.ds(0, LANE)] = down.T
     part_f[:, pl.ds(LANE, LANE)] = up_g.T
     own_rows = pl.multiple_of(offset + core * (per_chip // 2), 8)
@@ -361,7 +380,7 @@
     def _():
         pltpu.make_async_copy(outp, outp, c_send).wait()
 
-    for i, dst in enumerate((r_n, r_h, r_a, r_l)):
+    for i, dst in enumerate((r_n, r_h, r_a)):
         @pl.when(core == side)
         def _():
             whole = dst.at[pl.ds(0, (n_z - 1) * tok)]
@@ -424,10 +443,9 @@
                 pltpu.VMEM((tok, rank), F32),
                 pltpu.VMEM((tok, rank), BF16),
                 pltpu.VMEM((tok, rank), F32),
-                pltpu.VMEM((tok, rank), BF16),
+                pltpu.VMEM((tok // G, n_z, G, win + rank), BF16),
                 pltpu.VMEM((long, win), BF16),
-                pltpu.VMEM((long, win), BF16),
-                pltpu.VMEM((long, rank), BF16),
+                pltpu.VMEM((long, win + rank), BF16),
                 pltpu.VMEM((long, rank), BF16),
                 pltpu.VMEM((blocks, tok, cols), F32),
                 pltpu.VMEM((blocks, tok, cols), F32),
@@ -443,10 +461,10 @@
                 dma((2,)),
                 dma((pieces, CHUNKS)),
                 dma,
-                dma((4,)),
-                dma((4,)),
-                dma((4,)),
-                dma((4,)),
+                dma((3,)),
+                dma((3,)),
+                dma((3,)),
+                dma((3,)),
                 dma,
                 dma,
                 dma,

time: 136 us -> 130 us (0.956)
  the two profiles are of different devices: /device:TPU:17 before, /device:TPU:1 now
where the time goes in v2:
time: 130 us
  Pallas kernels  126 us (97%)
  local copies, waits for them, and re-layouts  3.63 us (3%)
    pallas_call x1, Pallas kernels, on_device(): pl.pallas_call(functools.partial(kernel, n_sec, n_dp), out_shape=(jax.Sha...  126 us
    unnamed x7, local copies, waits for them, and re-layouts  3.63 us

profile of v2, /device:TPU:1, one launch (start us, length us, event | category | flops | bytes accessed | tf_op | source)
XLA Modules:
  0.0 130.2 jit_solution(8500195983601079435)
XLA Ops:
  0.6 125.9 %shard_map.103 = (bf16[128,4608]{1,0:T(8,128)(2,1)}, f32[288,256]{1,0:T(8,128)}, f32[1,8]{1,0:T(1,128)}) custom-call(bf16[128,4608]{1,0:T(8,128)(2,1)} %bitcast.8, bf16[128,4608]{1,0:T(8,128)(2,1)} %bitcast.9, f32[1,4608]{1,0:T(1,128)} %refs_2_.1, bf16[4608,128]{1,0:T(8,128)(2,1)} %bitcast.10, bf16[4608,128]{1,0:T(8,128)(2,1)} %bitcast.11, ...), custom_call_target="tpu_custom_call" | custom-call | tf_op jit(solution)/shard_map/pallas_call | solution.py:422
  126.6 0.0 copy-start
  126.6 0.0 copy-start.1
  126.6 2.4 %copy.14 = bf16[1,1,128,4608]{3,2,1,0:T(8,128)(2,1)} copy(bf16[1,1,128,4608]{3,2,1,0:T(8,128)(2,1)} %bitcast.12) | data formatting | bytes 2359296
  129.0 0.0 copy-done
  129.0 0.7 copy.15
  129.7 0.0 copy-done.1
  129.7 0.5 copy.16
Async XLA Ops:
  126.6 2.4 %copy-start = (f32[288,256]{1,0:T(8,128)S(1)}, f32[288,256]{1,0:T(8,128)}, u32[]{:S(2)}) copy-start(f32[288,256]{1,0:T(8,128)} %get-tuple-element.7) | copy-start | bytes 884740
  126.6 3.1 %copy-start.1 = (f32[1,8]{1,0:T(1,128)S(1)}, f32[1,8]{1,0:T(1,128)}, u32[]{:S(2)}) copy-start(f32[1,8]{1,0:T(1,128)} %get-tuple-element.8) | copy-start | bytes 100

commit v3 on v2

--- a/solution.py
+++ b/solution.py
@@ -11,7 +11,9 @@
 NORM_EPS = 1e-06
 MESH = pl.DeviceIdType.MESH
 F32, BF16 = jnp.float32, jnp.bfloat16
-R = 8
+R = 4
+Q = 4
+L = 8
 G = 16
 LANE = 128
 CHUNKS = 3
@@ -26,17 +28,58 @@
     return lax.dot_general(a, b, (((1,), (1,)), ((), ())), preferred_element_type=F32)
 
 
-def halves(v, half):
-    return jnp.concatenate([v[:, :half], v[:, half:]], axis=0)
+def pick(top, bottom):
+    row = lax.broadcasted_iota(jnp.int32, top.shape, 0)
+    return jnp.where(row < R, top, bottom)
+
+
+def turn(v):
+    return pltpu.roll(v, R, 0)
+
+
+def pack(v, width):
+    a, b, c, d = [v[:, q * width:(q + 1) * width] for q in range(Q)]
+    first = jnp.concatenate([pick(a, turn(b)), pick(c, turn(d))], axis=0)
+    second = jnp.concatenate([pick(turn(a), b), pick(turn(c), d)], axis=0)
+    return first.astype(BF16), second.astype(BF16)
+
+
+def unpack(first, second):
+    first, second = first.astype(F32), second.astype(F32)
+    out = []
+    for h in range(Q // 2):
+        a, b = first[h * L:(h + 1) * L], second[h * L:(h + 1) * L]
+        out += [pick(a, turn(b)), pick(turn(a), b)]
+    return out
+
+
+def doubled(v):
+    w = turn(v)
+    return pick(v, w), pick(w, v)
+
+
+def fold(both):
+    t = [both[(q // 2) * L:(q // 2 + 1) * L, q * LANE:(q + 1) * LANE] for q in range(Q)]
+    y = pick(t[0], t[1]) + pick(t[2], t[3])
+    return y + turn(y)
+
+
+def widen(low):
+    zero = jnp.zeros_like(low)
+    upper, lower = pick(low, zero), pick(zero, low)
+    return jnp.concatenate([
+        jnp.concatenate([upper, lower, zero, zero], axis=1),
+        jnp.concatenate([zero, zero, upper, lower], axis=1),
+    ], axis=0).astype(BF16)
 
 
 def kernel(n_sec, n_dp, *refs):
     (acts, og, gains, dn, up, thr, lens, own, ig, lora, owned,
-     xv, flat, ucat, dv, dtc, normed, xp, arr, outp, outf, scale, hidf, hidb, lowf, stage,
-     r_n, r_a, r_h, nw, hw, parts, part_f, other, lora_v, hid_t, low_t, doc_row, doc_col,
-     s_load, s_out, s_chain, c_send, rs, rso, ss, sso, p_send, p_recv, o_send, o_recv) = refs
+     xv, flat, ucat, dv, dtc, normed, xp, arr, outp, scale, hidf, hidb, hidp, lowp, stage,
+     r_n, r_a, r_h, nw, hw, parts, part_f, other, hid_t, low_t, doc_row, doc_col,
+     s_load, s_chain, c_send, rs, rso, ss, sso, p_send, p_recv, o_send, o_recv) = refs
     tok, feat = xv.shape
-    half = feat // 2
+    width = feat // Q
     n_docs = lens.shape[1]
     pieces, groups = tok // R, tok // G
     n_z = n_dp // 2
@@ -45,7 +88,7 @@
     blocks = n_dp // 2
     span = blocks * tok
     cols = tok + tok // 2
-    lanes = half // CHUNKS
+    lanes = width // CHUNKS
 
     sec = lax.axis_index("section")
     me = lax.axis_index("dp")
@@ -58,18 +101,15 @@
     def load(src, dst, i):
         return pltpu.make_async_copy(src, dst, s_load.at[i])
 
-    loads = [
-        load(acts, xv, 0),
-        load(dn, dv, 1),
-        load(up.at[pl.ds(0, half)], ucat.at[:, pl.ds(0, LANE)], 2),
-        load(up.at[pl.ds(half, half)], ucat.at[:, pl.ds(LANE, LANE)], 3),
+    loads = [load(dn, dv, 0), load(acts, xv, 1)] + [
+        load(up.at[pl.ds(q * width, width)], ucat.at[:, pl.ds(q * LANE, LANE)], 2 + q) for q in range(Q)
     ]
     for c in loads:
         c.start()
 
     @pl.when(sec == last)
     def _():
-        load(og, flat, 4).start()
+        load(og, flat, 2 + Q).start()
 
     barrier = pltpu.get_barrier_semaphore()
 
@@ -95,48 +135,58 @@
             r[pl.ds(span, tok // 2), :] = jnp.zeros((tok // 2, r.shape[1]), BF16)
 
     loads[0].wait()
+
+    def turn_map(t, _):
+        here = pl.ds(pl.multiple_of(t * LANE, LANE), LANE)
+        for q in range(Q):
+            there = pl.ds(pl.multiple_of(t * LANE + q * width, LANE), LANE)
+            dtc[pl.ds(q * LANE, LANE), here] = (dv[there, :].astype(F32).T * gains[:, there]).astype(BF16)
+        return 0
+
+    lax.fori_loop(0, width // LANE, turn_map, 0)
+    loads[1].wait()
 
     def norm_group(q, _):
         rows = pl.ds(pl.multiple_of(q * G, G), G)
         v = xv[rows, :].astype(F32)
         s = lax.rsqrt(jnp.sum(v * v, axis=1, keepdims=True) / feat + NORM_EPS)
-        scale[rows, :] = jnp.broadcast_to(s, (G, LANE))
         normed[rows, :] = (v * s * gains[...]).astype(BF16)
-        xp[2 * q] = halves(v[:R], half).astype(BF16)
-        xp[2 * q + 1] = halves(v[R:], half).astype(BF16)
+        for h in range(G // L):
+            p = q * (G // R) + 2 * h
+            own_rows = slice(h * L, (h + 1) * L)
+            xp[p], xp[p + 1] = pack(v[own_rows], width)
+            scale[p], scale[p + 1] = doubled(jnp.broadcast_to(s[own_rows], (L, LANE)))
         return 0
 
     lax.fori_loop(0, groups, norm_group, 0)
-    loads[1].wait()
     hidf[...] = jnp.zeros_like(hidf)
 
-    def down_tile(t, _):
-        here = pl.ds(pl.multiple_of(t * LANE, LANE), LANE)
-        there = pl.ds(pl.multiple_of(t * LANE + half, LANE), LANE)
-        dtc[pl.ds(0, LANE), here] = (dv[here, :].astype(F32).T * gains[:, here]).astype(BF16)
-        dtc[pl.ds(LANE, LANE), here] = (dv[there, :].astype(F32).T * gains[:, there]).astype(BF16)
-        hidf[...] += dot(normed[:, here], dv[here, :]) + dot(normed[:, there], dv[there, :])
+    def down_part(t, _):
+        here = pl.ds(pl.multiple_of(t * (width // 3), LANE), width // 3)
+        hidf[...] += dot(normed[:, here], dv[here, :])
         return 0
 
-    lax.fori_loop(0, half // LANE, down_tile, 0)
+    lax.fori_loop(0, 3 * Q, down_part, 0)
     hidb[...] = hidf[...].astype(BF16)
+    for h in range(tok // L):
+        hidp[2 * h], hidp[2 * h + 1] = doubled(hidf[pl.ds(h * L, L), :])
 
     @pl.when(sec == last)
     def _():
-        load(og, flat, 4).wait()
-
-        def pack(q, _):
+        load(og, flat, 2 + Q).wait()
+
+        def pack_group(q, _):
             rows = pl.ds(pl.multiple_of(q * G, G), G)
             v = flat[rows, :].astype(F32)
-            arr[2 * q] = halves(v[:R], half).astype(BF16)
-            arr[2 * q + 1] = halves(v[R:], half).astype(BF16)
+            for h in range(G // L):
+                p = q * (G // R) + 2 * h
+                arr[p], arr[p + 1] = pack(v[h * L:(h + 1) * L], width)
             return 0
 
-        lax.fori_loop(0, groups, pack, 0)
-
-    loads[2].wait()
-    loads[3].wait()
-
+        lax.fori_loop(0, groups, pack_group, 0)
+
+    for c in loads[2:]:
+        c.wait()
     ends = jnp.where(sec > 0, 1, 0) + jnp.where(sec < last, 1, 0)
     pl.semaphore_wait(barrier, n_dp - 1 + ends)
 
@@ -172,17 +222,24 @@
         spread_own(zz)
         return 0
 
+    def whole_rows(src, q):
+        p = q * (G // R)
+        both = [unpack(src[p + 2 * h], src[p + 2 * h + 1]) for h in range(G // L)]
+        return [jnp.concatenate(x, axis=0) for x in zip(*both)]
+
     def spread_arriving(q):
         row = q * G
-        a, b = arr[2 * q].astype(F32), arr[2 * q + 1].astype(F32)
-        low = lowf[pl.ds(pl.multiple_of(row, G), G), :].astype(BF16)
+        quarters = whole_rows(arr, q)
+        p = q * (G // R)
+        low = jnp.concatenate(
+            [pick(lowp[p + 2 * h], lowp[p + 2 * h + 1]) for h in range(G // L)], axis=0).astype(BF16)
         lane = lax.broadcasted_iota(jnp.int32, (1, LANE), 1)
         for zz in range(n_z):
             first = per_chip * zz
             start = first // LANE * LANE
-            part = start // half
-            r0, l0 = part * R, start - part * half
-            w = jnp.concatenate([a[r0:r0 + R, l0:l0 + win], b[r0:r0 + R, l0:l0 + win]], axis=0)
+            part = start // width
+            l0 = start - part * width
+            w = quarters[part][:, l0:l0 + win]
             w = jnp.concatenate([
                 w[:, :LANE] * jnp.where(lane >= first - start, 1.0, 0.0),
                 w[:, LANE:win - LANE],
@@ -232,60 +289,51 @@
             device_id={"section": jnp.maximum(sec - 1, 0)}, device_id_type=MESH,
         )
 
-    def piece(p):
-        row = pl.multiple_of(p * R, R)
-        rows = pl.ds(row, R)
-        both = jnp.zeros((2 * R, 2 * LANE), F32)
-        for c in range(CHUNKS):
-            @pl.when(sec < last)
-            def _():
+    parts_of = [pl.ds(c * lanes, lanes) for c in range(CHUNKS)]
+
+    def piece(p, recv, send_on):
+        both = jnp.zeros((2 * L, Q * LANE), F32)
+        for c, there in enumerate(parts_of):
+            if recv:
                 chain_copy(p, c).wait_recv()
-
-            there = pl.ds(c * lanes, lanes)
             both += dot(arr[p, :, there], ucat[there, :])
-        low = (both[:R, :LANE] + both[R:, LANE:]).astype(BF16).astype(F32)
-        lowf[rows, :] = low
-        s = scale[rows, :1]
-        k = s * s * (jnp.sum(low * hidf[rows, :], axis=1, keepdims=True) / feat)
-        zero = jnp.zeros_like(low)
-        wide = jnp.concatenate(
-            [jnp.concatenate([low, zero], axis=1), jnp.concatenate([zero, low], axis=1)], axis=0
-        ).astype(BF16)
+        low = fold(both).astype(BF16).astype(F32)
+        s = scale[p][:, :1]
+        k = s * s * (jnp.sum(low * hidp[p], axis=1, keepdims=True) / feat)
         s2, k2 = jnp.concatenate([s, s], axis=0), jnp.concatenate([k, k], axis=0)
-        for c in range(CHUNKS):
-            there = pl.ds(c * lanes, lanes)
-            back = dot(wide, dtc[:, there])
-            out = arr[p, :, there].astype(F32) + s2 * back - k2 * xp[p, :, there].astype(F32)
+        wide = widen(low)
+        for c, there in enumerate(parts_of):
+            out = arr[p, :, there].astype(F32) + s2 * dot(wide, dtc[:, there]) - k2 * xp[p, :, there].astype(F32)
             outp[p, :, there] = out.astype(BF16)
-
-            @pl.when(sec > 0)
-            def _():
+            if send_on:
                 chain_copy(p, c).start()
-
-    def group(q, _):
-        piece(2 * q)
-        piece(2 * q + 1)
-        row = pl.multiple_of(q * G, G)
-        rows = pl.ds(row, G)
-
-        def unpack(src):
-            a, b = src[2 * q].astype(F32), src[2 * q + 1].astype(F32)
-            return (jnp.concatenate([a[:R], b[:R]], axis=0).astype(BF16),
-                    jnp.concatenate([a[R:], b[R:]], axis=0).astype(BF16))
-
-        lo, hi = unpack(outp)
-        outf[rows, pl.ds(0, half)] = lo
-        outf[rows, pl.ds(half, half)] = hi
+        lowp[p] = low
+
+    def group(q, kind):
+        for t in range(G // R):
+            piece(q * (G // R) + t, *kind)
         spread_arriving(q)
 
         @pl.when(jnp.logical_not(early))
         def _():
             spread_own(q)
 
-        pltpu.make_async_copy(outf.at[rows], ig.at[rows], s_out.at[0]).start()
-        return 0
-
-    lax.fori_loop(0, groups, group, 0)
+        rows = pl.ds(pl.multiple_of(q * G, G), G)
+        for part, v in enumerate(whole_rows(outp, q)):
+            ig[rows, pl.ds(part * width, width)] = v.astype(BF16)
+
+    def run(where, *kind):
+        @pl.when(where)
+        def _():
+            def step(q, _):
+                group(q, kind)
+                return 0
+
+            lax.fori_loop(0, groups, step, 0)
+
+    run(sec == last, False, True)
+    run((sec > 0) & (sec < last), True, True)
+    run(sec == 0, True, False)
 
     def arrived(dst, i):
         pltpu.make_async_copy(dst.at[pl.ds(0, span)], dst.at[pl.ds(0, span)], rs.at[i]).wait()
@@ -370,9 +418,7 @@
     owned[...] = jnp.sum(held, axis=0, keepdims=True)
 
     swap.wait()
-    lora_v[...] = (part_f[pl.ds(own_rows, per_chip // 2), :] + other[...]) / n_docs
-    store = pltpu.make_async_copy(lora_v, lora, s_out.at[1])
-    store.start()
+    lora[...] = (part_f[pl.ds(own_rows, per_chip // 2), :] + other[...]) / n_docs
 
     pltpu.make_async_copy(most, most, p_send).wait()
 
@@ -395,9 +441,6 @@
         def _():
             whole = dst.at[pl.ds(0, (n_z - 1) * (tok // 2))]
             pltpu.make_async_copy(whole, whole, sso.at[i]).wait()
-
-    pltpu.make_async_copy(outf, outf, s_out.at[0]).wait()
-    store.wait()
 
 
 def solution(mesh):
@@ -407,7 +450,7 @@
     def on_device(acts, output_gradient, gains, down, up, thresholds, lengths, owners):
         tok, feat = acts.shape[2:]
         rank = down.shape[2]
-        half = feat // 2
+        width = feat // Q
         per_chip = feat // n_z
         win = -(-per_chip // LANE) * LANE
         pieces, blocks = tok // R, n_dp // 2
@@ -417,32 +460,32 @@
         hbm = pl.BlockSpec(memory_space=pl.ANY)
         vmem = pl.BlockSpec(memory_space=pltpu.VMEM)
         dma = pltpu.SemaphoreType.DMA
-        packed = pltpu.VMEM((pieces, 2 * R, half), BF16)
+        packed = pltpu.VMEM((pieces, Q * R, width), BF16)
         whole = pltpu.VMEM((tok, feat), BF16)
         ig, lora, owned = pl.pallas_call(
             functools.partial(kernel, n_sec, n_dp),
             out_shape=(
-                jax.ShapeDtypeStruct((tok, feat), BF16),
-                jax.ShapeDtypeStruct((feat // n_dp, 2 * rank), F32),
-                jax.ShapeDtypeStruct((1, OWN), F32),
+                pltpu.VMEM((tok, feat), BF16),
+                pltpu.VMEM((feat // n_dp, 2 * rank), F32),
+                pltpu.VMEM((1, OWN), F32),
             ),
             in_specs=[hbm, hbm, vmem, hbm, hbm, vmem, vmem, vmem],
-            out_specs=(hbm, hbm, vmem),
+            out_specs=(vmem, vmem, vmem),
             scratch_shapes=[
                 whole,
                 whole,
-                pltpu.VMEM((half, 2 * rank), BF16),
+                pltpu.VMEM((width, Q * rank), BF16),
                 pltpu.VMEM((feat, rank), BF16),
-                pltpu.VMEM((2 * rank, half), BF16),
+                pltpu.VMEM((Q * rank, width), BF16),
                 whole,
                 packed,
                 packed,
                 packed,
-                whole,
-                pltpu.VMEM((tok, LANE), F32),
+                pltpu.VMEM((pieces, L, LANE), F32),
                 pltpu.VMEM((tok, rank), F32),
                 pltpu.VMEM((tok, rank), BF16),
-                pltpu.VMEM((tok, rank), F32),
+                pltpu.VMEM((pieces, L, rank), F32),
+                pltpu.VMEM((pieces, L, rank), F32),
                 pltpu.VMEM((tok // G, n_z, G, win + rank), BF16),
                 pltpu.VMEM((long, win), BF16),
                 pltpu.VMEM((long, win + rank), BF16),
@@ -452,13 +495,11 @@
                 pltpu.VMEM((n_dp, 8, LANE), F32),
                 pltpu.VMEM((win, 2 * rank), F32),
                 pltpu.VMEM((per_chip // 2, 2 * rank), F32),
-                pltpu.VMEM((per_chip // 2, 2 * rank), F32),
                 pltpu.VMEM((rank, span), F32),
                 pltpu.VMEM((rank, span), F32),
                 pltpu.VMEM((8, span + tok), F32),
                 pltpu.VMEM((span + tok, LANE), F32),
-                dma((5,)),
-                dma((2,)),
+                dma((3 + Q,)),
                 dma((pieces, CHUNKS)),
                 dma,
                 dma((3,)),

time: 130 us -> 120 us (0.923)
  Pallas kernels: 126 us -> 117 us
  local copies, waits for them, and re-layouts: 3.63 us -> 2.24 us
    pallas_call x1, Pallas kernels: 126 us -> 117 us  [on_device(): pl.pallas_call(functools.partial(kernel, n_sec, n_dp), out_shape=(pltpu.V...]
    unnamed x7 -> x3, local copies, waits for them, and re-layouts: 3.63 us -> 2.24 us
where the time goes in v3:
time: 120 us
  Pallas kernels  117 us (98%)
  local copies, waits for them, and re-layouts  2.24 us (2%)
    pallas_call x1, Pallas kernels, on_device(): pl.pallas_call(functools.partial(kernel, n_sec, n_dp), out_shape=(pltpu.V...  117 us

profile of v3, /device:TPU:1, one launch (start us, length us, event | category | flops | bytes accessed | tf_op | source)
XLA Modules:
  0.0 119.7 jit_solution(7511497558774899382)
XLA Ops:
  0.6 116.8 %shard_map.103 = (bf16[128,4608]{1,0:T(8,128)(2,1)S(1)}, f32[288,256]{1,0:T(8,128)S(1)}, f32[1,8]{1,0:T(1,128)S(1)}) custom-call(bf16[128,4608]{1,0:T(8,128)(2,1)} %bitcast.11, bf16[128,4608]{1,0:T(8,128)(2,1)} %bitcast.12, f32[1,4608]{1,0:T(1,128)} %refs_2_.1, bf16[4608,128]{1,0:T(8,128)(2,1)} %bitcast.13, bf16[4608,128]{1,0:T(8,128)(2,1)} %bitcast.14, ...), custom_call_target="tpu_custom_call" | custom-call | tf_op jit(solution)/shard_map/pallas_call | solution.py:465
  117.5 1.0 copy.14
  118.5 0.7 copy.15
  119.2 0.5 copy.16

commit v4 on v3

--- a/solution.py
+++ b/solution.py
@@ -17,7 +17,10 @@
 G = 16
 LANE = 128
 CHUNKS = 3
-LATE = 2
+PASSED, AWAY = 3, 12
+PASS_GROUPS = 5
+ORDER = (4, 3, 5, 2, 6, 1, 7, 0)
+LATE = 1
 
 
 def dot(a, b):
@@ -75,9 +78,9 @@
 
 def kernel(n_sec, n_dp, *refs):
     (acts, og, gains, dn, up, thr, lens, own, ig, lora, owned,
-     xv, flat, ucat, dv, dtc, normed, xp, arr, outp, scale, hidf, hidb, hidp, lowp, stage,
+     xv, flat, ucat, dv, dtc, normed, xp, arr, outp, scale, hidf, hidb, hidp, lowp, stage, passing_by,
      r_n, r_a, r_h, nw, hw, parts, part_f, other, hid_t, low_t, doc_row, doc_col,
-     s_load, s_chain, c_send, rs, rso, ss, sso, p_send, p_recv, o_send, o_recv) = refs
+     s_load, s_chain, c_send, rs, rso, ss, sso, p_send, p_recv, o_send, o_recv, by_send, by_recv) = refs
     tok, feat = xv.shape
     width = feat // Q
     n_docs = lens.shape[1]
@@ -129,6 +132,19 @@
         def _():
             greet({"dp": peer})
 
+    opposite = lax.rem(z + n_z // 2, n_z)
+    passed = sec < PASSED
+    passing = (sec >= AWAY) & (sec < AWAY + PASSED)
+
+    @pl.when(passing)
+    def _():
+        greet({"section": sec - AWAY})
+
+    @pl.when(passed & (core == opposite * 2 // n_z))
+    def _():
+        for c in range(2):
+            greet({"section": sec + AWAY, "dp": 2 * opposite + c})
+
     @pl.when(core == 1)
     def _():
         for r in (r_n, r_a, r_h):
@@ -188,35 +204,43 @@
     for c in loads[2:]:
         c.wait()
     ends = jnp.where(sec > 0, 1, 0) + jnp.where(sec < last, 1, 0)
-    pl.semaphore_wait(barrier, n_dp - 1 + ends)
-
-    def send(src, dst, i, zz, dest_core, row, n, sems):
-        at = pl.multiple_of(row, G)
-        d = dst.at[pl.ds(at, n), :]
+    extra = jnp.where(passed | passing, 1, 0)
+    pl.semaphore_wait(barrier, n_dp - 1 + ends + extra)
+
+    def send(src, dst, i, zz, dest_core, row, n, sems, other_chip):
+        d = dst.at[pl.ds(pl.multiple_of(row, G), n), :]
         dest = 2 * zz + dest_core
 
-        @pl.when(dest == me)
-        def _():
-            pltpu.make_async_copy(src, d, sems[1].at[i]).start()
-
-        @pl.when(dest != me)
-        def _():
+        def remote():
             pltpu.make_async_remote_copy(
                 src_ref=src, dst_ref=d, send_sem=sems[0].at[i], recv_sem=sems[1].at[i],
                 device_id={"dp": dest}, device_id_type=MESH,
             ).start()
 
-    def spread_own(zz):
+        if other_chip is True:
+            remote()
+            return
+
+        @pl.when(dest == me)
+        def _():
+            pltpu.make_async_copy(src, d, sems[1].at[i]).start()
+
+        @pl.when(dest != me)
+        def _():
+            remote()
+
+    def spread_own(turn_of):
+        zz = lax.rem(z + turn_of, n_z)
         start = pl.multiple_of(per_chip * zz // LANE * LANE, LANE)
         there = pl.ds(start, win)
-        send(normed.at[:, there], r_n, 0, zz, side, slot * tok, tok, (ss, rs))
-        send(hidb, r_h, 1, zz, side, slot * tok, tok, (ss, rs))
+        send(normed.at[:, there], r_n, 0, zz, side, slot * tok, tok, (ss, rs), None)
+        send(hidb, r_h, 1, zz, side, slot * tok, tok, (ss, rs), None)
 
         @pl.when(me == blocks)
         def _():
             top = pl.ds(0, tok // 2)
-            send(normed.at[top, there], r_n, 0, zz, 0, span, tok // 2, (sso, rso))
-            send(hidb.at[top], r_h, 1, zz, 0, span, tok // 2, (sso, rso))
+            send(normed.at[top, there], r_n, 0, zz, 0, span, tok // 2, (sso, rso), None)
+            send(hidb.at[top], r_h, 1, zz, 0, span, tok // 2, (sso, rso), None)
 
     def spread_all(zz, _):
         spread_own(zz)
@@ -247,12 +271,28 @@
             ], axis=1)
             stage[q, zz, :, pl.ds(0, win)] = w.astype(BF16)
             stage[q, zz, :, pl.ds(win, LANE)] = low
-        for zz in range(n_z):
-            send(stage.at[q, zz], r_a, 2, zz, side, slot * tok + row, G, (ss, rs))
+        for k in ORDER:
+            zz = lax.rem(z + k, n_z)
+            src = stage.at[q, zz]
+            if 2 * k == n_z:
+                direct = jnp.logical_not(passed & (q < PASS_GROUPS))
+
+                @pl.when(direct)
+                def _():
+                    send(src, r_a, 2, zz, side, slot * tok + row, G, (ss, rs), True)
+
+                @pl.when(jnp.logical_not(direct))
+                def _():
+                    pltpu.make_async_remote_copy(
+                        src_ref=src, dst_ref=passing_by.at[q], send_sem=ss.at[2], recv_sem=by_recv.at[q],
+                        device_id={"section": sec + AWAY}, device_id_type=MESH,
+                    ).start()
+            else:
+                send(src, r_a, 2, zz, side, slot * tok + row, G, (ss, rs), k != 0)
 
             @pl.when((me == blocks) & (row < tok // 2))
             def _():
-                send(stage.at[q, zz], r_a, 2, zz, 0, span + lax.rem(row, tok // 2), G, (sso, rso))
+                send(src, r_a, 2, zz, 0, span + lax.rem(row, tok // 2), G, (sso, rso), k != 0)
 
     def doc_tables():
         k_row = lax.broadcasted_iota(jnp.int32, (n_docs, n_docs), 1)
@@ -361,6 +401,20 @@
         nw[b] = weight * dot_nt(mine(r_n, b), r_n[there, :])
         hw[b] = weight * dot_nt(r_h[pl.ds(b * tok, tok), :], r_h[there, :])
         hid_t[:, pl.ds(b * tok, tok)] = r_h[pl.ds(b * tok, tok), :].astype(F32).T
+
+    @pl.when(passing)
+    def _():
+        def pass_on(q, _):
+            block = passing_by.at[q]
+            pltpu.make_async_copy(block, block, by_recv.at[q]).wait()
+            at = pl.multiple_of(slot * tok + q * G, G)
+            pltpu.make_async_remote_copy(
+                src_ref=block, dst_ref=r_a.at[pl.ds(at, G), :], send_sem=by_send, recv_sem=rs.at[2],
+                device_id={"section": sec - AWAY, "dp": 2 * opposite + side}, device_id_type=MESH,
+            ).start()
+            return 0
+
+        lax.fori_loop(0, PASS_GROUPS, pass_on, 0)
 
     arrived(r_a, 2)
     win_l, low_l = pl.ds(0, win), pl.ds(win, LANE)
@@ -425,6 +479,11 @@
     @pl.when(sec > 0)
     def _():
         pltpu.make_async_copy(outp, outp, c_send).wait()
+
+    @pl.when(passing)
+    def _():
+        some = passing_by.at[pl.ds(0, PASS_GROUPS)]
+        pltpu.make_async_copy(some, some, by_send).wait()
 
     for i, dst in enumerate((r_n, r_h, r_a)):
         @pl.when(core == side)
@@ -487,6 +546,7 @@
                 pltpu.VMEM((pieces, L, rank), F32),
                 pltpu.VMEM((pieces, L, rank), F32),
                 pltpu.VMEM((tok // G, n_z, G, win + rank), BF16),
+                pltpu.VMEM((tok // G, G, win + rank), BF16),
                 pltpu.VMEM((long, win), BF16),
                 pltpu.VMEM((long, win + rank), BF16),
                 pltpu.VMEM((long, rank), BF16),
@@ -510,6 +570,8 @@
                 dma,
                 dma,
                 dma,
+                dma,
+                dma((tok // G,)),
             ],
             compiler_params=pltpu.CompilerParams(
                 collective_id=0, has_side_effects=True, vmem_limit_bytes=56 << 20

time: 120 us -> 115 us (0.958)
  Pallas kernels: 117 us -> 112 us
    pallas_call x1, Pallas kernels: 117 us -> 112 us  [on_device(): pl.pallas_call(functools.partial(kernel, n_sec, n_dp), out_shape=(pltpu.V...]
where the time goes in v4:
time: 115 us
  Pallas kernels  112 us (97%)
  local copies, waits for them, and re-layouts  2.24 us (2%)
    pallas_call x1, Pallas kernels, on_device(): pl.pallas_call(functools.partial(kernel, n_sec, n_dp), out_shape=(pltpu.V...  112 us

profile of v4, /device:TPU:1, one launch (start us, length us, event | category | flops | bytes accessed | tf_op | source)
XLA Modules:
  0.0 115.3 jit_solution(14864193844726429530)
XLA Ops:
  0.6 112.4 %shard_map.103 = (bf16[128,4608]{1,0:T(8,128)(2,1)S(1)}, f32[288,256]{1,0:T(8,128)S(1)}, f32[1,8]{1,0:T(1,128)S(1)}) custom-call(bf16[128,4608]{1,0:T(8,128)(2,1)} %bitcast.11, bf16[128,4608]{1,0:T(8,128)(2,1)} %bitcast.12, f32[1,4608]{1,0:T(1,128)} %refs_2_.1, bf16[4608,128]{1,0:T(8,128)(2,1)} %bitcast.13, bf16[4608,128]{1,0:T(8,128)(2,1)} %bitcast.14, ...), custom_call_target="tpu_custom_call" | custom-call | tf_op jit(solution)/shard_map/pallas_call | solution.py:524
  113.1 1.0 copy.14
  114.1 0.7 copy.15
  114.8 0.5 copy.16

commit v5 on v4

--- a/solution.py
+++ b/solution.py
@@ -191,15 +191,12 @@
     def _():
         load(og, flat, 2 + Q).wait()
 
-        def pack_group(q, _):
-            rows = pl.ds(pl.multiple_of(q * G, G), G)
-            v = flat[rows, :].astype(F32)
-            for h in range(G // L):
-                p = q * (G // R) + 2 * h
-                arr[p], arr[p + 1] = pack(v[h * L:(h + 1) * L], width)
-            return 0
-
-        lax.fori_loop(0, groups, pack_group, 0)
+    def pack_group(q):
+        rows = pl.ds(pl.multiple_of(q * G, G), G)
+        v = flat[rows, :].astype(F32)
+        for h in range(G // L):
+            p = q * (G // R) + 2 * h
+            arr[p], arr[p + 1] = pack(v[h * L:(h + 1) * L], width)
 
     for c in loads[2:]:
         c.wait()
@@ -350,6 +347,8 @@
         lowp[p] = low
 
     def group(q, kind):
+        if not kind[0]:
+            pack_group(q)
         for t in range(G // R):
             piece(q * (G // R) + t, *kind)
         spread_arriving(q)

time: 115 us -> 115 us (level)
  no operation moved by 1% of the time
where the time goes in v5:
time: 115 us
  Pallas kernels  112 us (97%)
  local copies, waits for them, and re-layouts  2.24 us (2%)
    pallas_call x1, Pallas kernels, on_device(): pl.pallas_call(functools.partial(kernel, n_sec, n_dp), out_shape=(pltpu.V...  112 us

profile of v5, /device:TPU:1, one launch (start us, length us, event | category | flops | bytes accessed | tf_op | source)
XLA Modules:
  0.0 115.1 jit_solution(5628349020062577560)
XLA Ops:
  0.6 112.2 %shard_map.103 = (bf16[128,4608]{1,0:T(8,128)(2,1)S(1)}, f32[288,256]{1,0:T(8,128)S(1)}, f32[1,8]{1,0:T(1,128)S(1)}) custom-call(bf16[128,4608]{1,0:T(8,128)(2,1)} %bitcast.11, bf16[128,4608]{1,0:T(8,128)(2,1)} %bitcast.12, f32[1,4608]{1,0:T(1,128)} %refs_2_.1, bf16[4608,128]{1,0:T(8,128)(2,1)} %bitcast.13, bf16[4608,128]{1,0:T(8,128)(2,1)} %bitcast.14, ...), custom_call_target="tpu_custom_call" | custom-call | tf_op jit(solution)/shard_map/pallas_call | solution.py:523
  112.8 1.0 copy.14
  113.8 0.7 copy.15
  114.6 0.5 copy.16
